TPU v7x, 128 devices: a whole 4x4x4 slice. The times are simulated.
128 devices in a mesh: ops: 8 (over x, core), sec: 16 (over y, z).
Axes of the slice: x: 4, y: 4, z: 4, core: 2. Of those that a mesh axis runs over, the one named last changes fastest.
Arguments:
- psi: bfloat16 [16, 16, 512, 512], P(None, 'sec'), may hold values from -6 to 6
- left_ops: bfloat16 [8, 16, 512, 512], P('ops'), may hold values from -0.25 to 0.25
- left_src: int32 [8, 16], P('ops'), may hold values from 0 to 15
- right_ops: bfloat16 [8, 16, 512, 512], P('ops'), may hold values from -0.125 to 0.125
- right_src: int32 [8, 16], P('ops'), may hold values from 0 to 15
- left_parity: int32 [16], replicated, may hold values from 0 to 1
- right_parity: int32 [16], replicated, may hold values from 0 to 1
Outputs:
- sigma: bfloat16 [16, 16, 512, 512], P('sec', 'ops')
All inputs are finite; a program needn't handle non-finite values.
Results may differ from a plain program's by a relative error of at most 0.015.
Values may be sent and summed in bfloat16 or wider, within the bound.
No kernel may reach another device: no remote copies, remote signals or barrier semaphores. Data moves between devices by JAX's collectives and lax.ppermute only.
A program may use at most 128 MiB of HBM per device.

v0:
```python
import jax
import jax.numpy as jnp
from jax import lax
from jax.sharding import PartitionSpec as P


def local(psi, left_ops, left_src, right_ops, right_src, left_parity, right_parity):
    col_count = psi.shape[1]
    sector_total = psi.shape[0]
    sec_index = lax.axis_index("sec")
    ops_index = lax.axis_index("ops")
    col_parity = lax.dynamic_slice_in_dim(right_parity, sec_index * col_count, col_count)
    live_cols = (left_parity[:, None] + col_parity[None, :]) % 2 == 1
    masked = jnp.where(live_cols[:, :, None, None], psi, jnp.zeros_like(psi))
    source_rows = jnp.take(masked, left_src, axis=0)
    contracted = jnp.einsum(
        "giab,gikbc->gikac", left_ops, source_rows, preferred_element_type=jnp.float32
    ).astype(jnp.bfloat16)
    relayed = lax.all_to_all(contracted, "sec", split_axis=1, concat_axis=2, tiled=True)

    def take_columns(column_block, column_index):
        return jnp.take(column_block, column_index, axis=1)

    kept_rows = sector_total // lax.axis_size("ops")
    picked = jax.vmap(take_columns)(relayed, right_src)
    summed = lax.psum_scatter(
        jnp.einsum(
            "gikab,gkcb->kiac", picked, right_ops, preferred_element_type=jnp.float32
        ).astype(jnp.bfloat16),
        "ops",
        scatter_dimension=0,
        tiled=True,
    ).astype(jnp.float32)
    row_parity = lax.dynamic_slice_in_dim(left_parity, sec_index * col_count, col_count)
    out_parity = lax.dynamic_slice_in_dim(right_parity, ops_index * kept_rows, kept_rows)
    live_out = (out_parity[:, None] + row_parity[None, :]) % 2 == 1
    result = jnp.where(live_out[:, :, None, None], summed, jnp.zeros_like(summed))
    return jnp.transpose(result, (1, 0, 2, 3)).astype(jnp.bfloat16)


def solution(mesh):
    placed = (
        P(None, "sec", None, None),
        P("ops", None, None, None),
        P("ops", None),
        P("ops", None, None, None),
        P("ops", None),
        P(),
        P(),
    )
    return jax.shard_map(
        local, mesh=mesh, in_specs=placed, out_specs=P("sec", "ops", None, None), check_vma=False
    )
```

profile of v0, /device:TPU:1, one launch (start us, length us, event | category | flops | bytes accessed | tf_op | source)
XLA Modules:
  0.0 290.1 jit_solution(3799304770546401373)
XLA Ops:
  6.5 0.7 fusion.27
  7.2 0.7 and_bitcast_fusion
  7.9 1.2 dynamic_slice.11
  9.1 1.3 fusion.21
  10.4 7.2 %fusion.4 = bf16[16,512,512]{2,1,0:T(8,128)(2,1)} fusion(bf16[16,1,512,512]{3,2,1,0:T(8,128)(2,1)} %param.7, pred[16]{0:T(512)(128)(4,1)S(1)} %fusion.21), kind=kLoop, calls=%fused_computation.7 | loop fusion | flops 4194304 | bytes 16777232 | tf_op jit(solution)/shard_map/jit(_where)/select_n | solution.py:14
  17.6 8.1 %gather_fusion = bf16[16,512,512]{2,1,0:T(8,128)(2,1)} fusion(bf16[16,512,512]{2,1,0:T(8,128)(2,1)} %fusion.4, s32[1024]{0:T(1024)S(1)} %pad_clamp_fusion), kind=kCustom, calls=%fused_computation | custom fusion | bytes 16777280 | tf_op jit(solution)/shard_map/jit(_take)/gather | solution.py:15
  25.7 11.8 %convert_bitcast_fusion.1 = bf16[1,16,1,512,512]{3,4,2,0,1:T(8,128)(2,1)} fusion(bf16[1,16,512,512]{3,2,1,0:T(8,128)(2,1)} %param.8, bf16[16,512,512]{2,1,0:T(8,128)(2,1)} %gather_fusion, pred[16]{0:T(512)(128)(4,1)S(1)} %and_bitcast_fusion), kind=kOutput, calls=%fused_computation.10 | convolution fusion | flops 4303355904 | bytes 25165840 | tf_op jit(solution)/shard_map/giab,gikbc->gikac/dot_general | solution.py:16
  37.5 0.0 copy-start.1
  37.5 8.8 %all-to-all-start = ((bf16[1,16,1,512,512]{3,4,2,0,1:T(8,128)(2,1)}), bf16[1,16,1,512,512]{3,4,2,0,1:T(8,128)(2,1)}, u32[]{:S(2)}, u32[]{:S(2)}) async-start(bf16[1,16,1,512,512]{3,4,2,0,1:T(8,128)(2,1)} %convert_bitcast_fusion.1), calls=%async_computation | async-start | bytes 16777216 | tf_op jit(solution)/shard_map/all_to_all | solution.py:19
  46.3 0.0 reduce-scatter.2.cloned.1.call-start
  46.3 0.0 copy-done.1
  46.4 145.9 %all-to-all-done = bf16[1,16,1,512,512]{3,4,2,0,1:T(8,128)(2,1)} async-done(((bf16[1,16,1,512,512]{3,4,2,0,1:T(8,128)(2,1)}), bf16[1,16,1,512,512]{3,4,2,0,1:T(8,128)(2,1)}, u32[]{:S(2)}, u32[]{:S(2)}) %all-to-all-start) | async-done | bytes 8388640 | tf_op jit(solution)/shard_map/all_to_all | solution.py:19
  192.3 12.3 %copy.18 = bf16[1,16,1,512,512]{4,3,1,2,0:T(8,128)(2,1)} copy(bf16[1,16,1,512,512]{3,4,2,0,1:T(8,128)(2,1)} %all-to-all-done) | data formatting | bytes 16777216 | tf_op jit(solution)/shard_map/all_to_all | solution.py:19
  204.6 8.2 %gather_fusion.1 = bf16[16,512,512]{2,1,0:T(8,128)(2,1)} fusion(bf16[1,16,512,512]{3,2,1,0:T(8,128)(2,1)} %bitcast.41, s32[16]{0:T(128)S(1)} %or_bitcast_fusion), kind=kCustom, calls=%fused_computation.1 | custom fusion | bytes 16777344 | tf_op jit(solution)/shard_map/vmap(jit(_take))/gather | solution.py:22
  212.8 11.4 %convert_bitcast_fusion = bf16[16,1,512,512]{3,2,0,1:T(8,128)(2,1)} fusion(bf16[1,16,512,512]{3,2,1,0:T(8,128)(2,1)} %param.10, bf16[16,512,512]{2,1,0:T(8,128)(2,1)} %gather_fusion.1, pred[16]{0:T(512)(128)(4,1)S(1)} %and_bitcast_fusion.1), kind=kOutput, calls=%fused_computation.8 | convolution fusion | flops 4303355904 | bytes 25165840 | tf_op jit(solution)/shard_map/gikab,gkcb->kiac/dot_general | solution.py:27
  224.2 0.0 copy-start.2
  224.2 0.0 copy-start
  224.2 0.0 reduce-scatter.2.cloned.1.call-update
  224.2 0.6 copy-done.2
  224.9 0.6 dynamic_slice.10
  225.4 0.0 copy-done
  225.4 0.7 fusion.20
  226.2 54.5 %reduce-scatter.2.cloned.1.call-done = bf16[2,1,512,512]{3,2,0,1:T(8,128)(2,1)} async-done(((bf16[16,1,512,512]{3,2,0,1:T(8,128)(2,1)}), bf16[2,1,512,512]{3,2,0,1:T(8,128)(2,1)}) %reduce-scatter.2.cloned.1.call-update) | async-done | bytes 1048592 | tf_op jit(solution)/shard_map/reduce_scatter | solution.py:26
  280.7 2.5 fusion.19
  (5 shorter events, 0.0 us)
Async XLA Ops:
  37.5 8.8 %copy-start.1 = (s32[1,16]{1,0:T(1,128)S(1)}, s32[1,16]{1,0:T(1,128)}, u32[]{:S(2)}) copy-start(s32[1,16]{1,0:T(1,128)} %param.11) | copy-start | bytes 196
  37.5 154.8 %all-to-all-start = ((bf16[1,16,1,512,512]{3,4,2,0,1:T(8,128)(2,1)}), bf16[1,16,1,512,512]{3,4,2,0,1:T(8,128)(2,1)}, u32[]{:S(2)}, u32[]{:S(2)}) async-start(bf16[1,16,1,512,512]{3,4,2,0,1:T(8,128)(2,1)} %convert_bitcast_fusion.1), calls=%async_computation | async-start | bytes 16777216 | tf_op jit(solution)/shard_map/all_to_all | solution.py:19
  46.3 234.4 %reduce-scatter.2.cloned.1.call-start = ((), (), s32[]{:S(2)}) async-start(), calls=%async_computation.2 | async-start | bytes 9437184 | tf_op jit(solution)/shard_map/reduce_scatter | solution.py:26
  224.2 0.7 copy-start.2
  224.2 1.2 copy-start
Sparse Core Ops, SparseCore 0:
  224.3 56.3 reduce-scatter.1
where the time goes:
time: 291 us; the launch traced here: 290 us
  waiting for transfers between devices  200 us (69%)
  local copies, waits for them, and re-layouts  31.1 us (11%)
  matrix products  23.2 us (8%)
  between operations  13.5 us (5%)
  other arithmetic  13.1 us (5%)
  starting transfers between devices  8.82 us (3%)
    all_to_all x1, waiting for transfers between devices, local(): lax.all_to_all(contracted, 'sec', split_axis=1, concat_axis=2, tiled=True)  146 us
    reduce_scatter x1, waiting for transfers between devices, local(): lax.psum_scatter(jnp.einsum('gikab,gkcb->kiac', picked, right_ops, prefer...  54.5 us
    all_to_all x1, local copies, waits for them, and re-layouts, local(): lax.all_to_all(contracted, 'sec', split_axis=1, concat_axis=2, tiled=True)  12.3 us
    dot_general x1, matrix products, local(): jnp.einsum('giab,gikbc->gikac', left_ops, source_rows, preferred_element_...  11.8 us
    dot_general x1, matrix products, local(): jnp.einsum('gikab,gkcb->kiac', picked, right_ops, preferred_element_type=...  11.4 us
    all_to_all x1, starting transfers between devices, local(): lax.all_to_all(contracted, 'sec', split_axis=1, concat_axis=2, tiled=True)  8.78 us
    gather x2, local copies, waits for them, and re-layouts, take_columns(): return jnp.take(column_block, column_index, axis=1)  8.17 us
    gather x1, local copies, waits for them, and re-layouts, local(): source_rows = jnp.take(masked, left_src, axis=0)  8.12 us
  transfers between devices with their start and end apart: 2, of which 2 were waited for; matrix products, arithmetic and copies ran while one was open for 0% of the time, Pallas kernels for 0%

commit v1 on v0

v1 whole, which is shorter than its diff:
```python
import jax
import jax.numpy as jnp
from jax import lax
from jax.experimental import pallas as pl
from jax.experimental.pallas import tpu as pltpu
from jax.sharding import PartitionSpec as P

CHUNKS = (320, 192)
F32 = jnp.float32
BF16 = jnp.bfloat16
MIB = 1024 * 1024


def left_kernel(me, ls, rs, lp, rp, psi, left, *rest):
    outs = rest[: len(CHUNKS)]
    items, pbuf, lbuf, obuf, psem, lsem, osem = rest[len(CHUNKS):]
    sectors = psi.shape[0]
    col = me[0]
    col_parity = rp[col] & 1

    def scan(k, flags):
        hit = (rs[k] == col).astype(jnp.int32)
        odd = rp[k] & 1
        return flags[0] | (hit * odd), flags[1] | (hit * (1 - odd))

    for_even, for_odd = lax.fori_loop(0, sectors, scan, (jnp.int32(0), jnp.int32(0)))

    def fetch(i, count):
        source = ls[i]
        wanted = jnp.where((lp[i] & 1) == 1, for_odd, for_even)
        need = (wanted == 1) & ((lp[source] & 1) != col_parity)

        @pl.when(need)
        def _():
            items[count] = i
            pltpu.make_async_copy(psi.at[source], pbuf.at[count], psem.at[count]).start()
            pltpu.make_async_copy(left.at[i], lbuf.at[count], lsem.at[count]).start()

        return count + need.astype(jnp.int32)

    count = lax.fori_loop(0, sectors, fetch, jnp.int32(0))

    def stores(j):
        at = 0
        for c, rows in enumerate(CHUNKS):
            yield pltpu.make_async_copy(
                obuf.at[j, pl.ds(at, rows)], outs[c].at[items[j]], osem.at[c, j]
            )
            at += rows

    def work(j, carry):
        pltpu.make_async_copy(psi.at[0], pbuf.at[j], psem.at[j]).wait()
        pltpu.make_async_copy(left.at[0], lbuf.at[j], lsem.at[j]).wait()
        obuf[j] = jnp.dot(lbuf[j], pbuf[j], preferred_element_type=F32).astype(BF16)
        for copy in stores(j):
            copy.start()
        return carry

    lax.fori_loop(0, count, work, 0)

    def finish(j, carry):
        for copy in stores(j):
            copy.wait()
        return carry

    lax.fori_loop(0, count, finish, 0)


def left_products(me, ls, rs, lp, rp, psi, left):
    k, m = psi.shape[0], psi.shape[-1]
    smem = pl.BlockSpec(memory_space=pltpu.SMEM)
    hbm = pl.BlockSpec(memory_space=pl.ANY)
    return pl.pallas_call(
        left_kernel,
        out_shape=[jax.ShapeDtypeStruct((k, rows, m), BF16) for rows in CHUNKS],
        in_specs=[smem] * 5 + [hbm] * 2,
        out_specs=[hbm] * len(CHUNKS),
        scratch_shapes=[
            pltpu.SMEM((k,), jnp.int32),
            pltpu.VMEM((k, m, m), BF16),
            pltpu.VMEM((k, m, m), BF16),
            pltpu.VMEM((k, m, m), BF16),
            pltpu.SemaphoreType.DMA((k,)),
            pltpu.SemaphoreType.DMA((k,)),
            pltpu.SemaphoreType.DMA((len(CHUNKS), k)),
        ],
        compiler_params=pltpu.CompilerParams(vmem_limit_bytes=40 * MIB),
        cost_estimate=pl.CostEstimate(
            flops=8 * m ** 3, bytes_accessed=12 * m * m * 2, transcendentals=0
        ),
        name="left_products",
    )(me, ls, rs, lp, rp, psi, left)


def right_kernel(me, ls, rs, lp, rp, block, right, keep, give, items, zbuf, sbuf, rbuf, obuf, ssem, rsem, osem, zsem):
    sectors = right.shape[0]
    row, core = me[0], me[1]
    row_parity = lp[row] & 1
    source_parity = lp[ls[row]] & 1

    def fetch(k, count):
        live = (rp[k] & 1) != row_parity
        source = rs[k]
        need = live & ((rp[source] & 1) != source_parity)

        @pl.when(need)
        def _():
            items[count] = k
            pltpu.make_async_copy(block.at[source], sbuf.at[count], ssem.at[count]).start()
            pltpu.make_async_copy(right.at[k], rbuf.at[count], rsem.at[count]).start()

        return count + need.astype(jnp.int32)

    count = lax.fori_loop(0, sectors, fetch, jnp.int32(0))

    def place(buf, k, sem, act):
        slot = (k // 4) * 2 + k % 2
        mine = (k // 2) % 2 == core

        @pl.when(mine)
        def _():
            act(pltpu.make_async_copy(buf, keep.at[slot], sem))

        @pl.when(jnp.logical_not(mine))
        def _():
            act(pltpu.make_async_copy(buf, give.at[slot], sem))

    zbuf[...] = jnp.zeros_like(zbuf)

    def empty(k):
        return ((rp[k] & 1) != row_parity) & ((rp[rs[k]] & 1) == source_parity)

    def clear(k, carry):
        @pl.when(empty(k))
        def _():
            place(zbuf, k, zsem.at[k], lambda copy: copy.start())

        return carry

    lax.fori_loop(0, sectors, clear, 0)

    def work(j, carry):
        pltpu.make_async_copy(block.at[0], sbuf.at[j], ssem.at[j]).wait()
        pltpu.make_async_copy(right.at[0], rbuf.at[j], rsem.at[j]).wait()
        obuf[j] = lax.dot_general(
            sbuf[j], rbuf[j], (((1,), (1,)), ((), ())), preferred_element_type=F32
        ).astype(BF16)
        place(obuf.at[j], items[j], osem.at[j], lambda copy: copy.start())
        return carry

    lax.fori_loop(0, count, work, 0)

    def finish(j, carry):
        place(obuf.at[j], items[j], osem.at[j], lambda copy: copy.wait())
        return carry

    lax.fori_loop(0, count, finish, 0)

    def cleared(k, carry):
        @pl.when(empty(k))
        def _():
            place(zbuf, k, zsem.at[k], lambda copy: copy.wait())

        return carry

    lax.fori_loop(0, sectors, cleared, 0)


def right_products(me, ls, rs, lp, rp, block, right):
    k, rows, m = block.shape
    smem = pl.BlockSpec(memory_space=pltpu.SMEM)
    hbm = pl.BlockSpec(memory_space=pl.ANY)
    half = jax.ShapeDtypeStruct((k // 2, rows, m), BF16)
    return pl.pallas_call(
        right_kernel,
        out_shape=[half, half],
        in_specs=[smem] * 5 + [hbm] * 2,
        out_specs=[hbm] * 2,
        scratch_shapes=[
            pltpu.SMEM((k,), jnp.int32),
            pltpu.VMEM((rows, m), BF16),
            pltpu.VMEM((k, rows, m), BF16),
            pltpu.VMEM((k, m, m), BF16),
            pltpu.VMEM((k, rows, m), BF16),
            pltpu.SemaphoreType.DMA((k,)),
            pltpu.SemaphoreType.DMA((k,)),
            pltpu.SemaphoreType.DMA((k,)),
            pltpu.SemaphoreType.DMA((k,)),
        ],
        compiler_params=pltpu.CompilerParams(vmem_limit_bytes=40 * MIB),
        cost_estimate=pl.CostEstimate(
            flops=16 * rows * m * m, bytes_accessed=8 * m * m * 2 + 16 * rows * m * 2, transcendentals=0
        ),
        name="right_products",
    )(me, ls, rs, lp, rp, block, right)


def summed_over_ops(keep, give):
    n = 8
    got = lax.ppermute(give, "ops", [(o, o ^ 1) for o in range(n)])
    pair = (keep.astype(F32) + got.astype(F32)).astype(BF16)
    chip = lax.axis_index("ops") // 2
    total = lax.dynamic_slice_in_dim(pair, chip * 2, 2).astype(F32)
    for hop in (1, 2, 3):
        part = lax.dynamic_slice_in_dim(pair, (chip + hop) % 4 * 2, 2)
        part = lax.ppermute(part, "ops", [(o, (o + 2 * hop) % n) for o in range(n)])
        total = total + part.astype(F32)
    return total


def local(psi, left_ops, left_src, right_ops, right_src, left_parity, right_parity):
    sec, ops = lax.axis_index("sec"), lax.axis_index("ops")
    me = jnp.stack([sec, ops % 2]).astype(jnp.int32)
    ls, rs = left_src[0], right_src[0]
    sends = left_products(me, ls, rs, left_parity, right_parity, psi[:, 0], left_ops[0])
    sums = []
    for send in sends:
        block = lax.all_to_all(send, "sec", 0, 0, tiled=True)
        keep, give = right_products(me, ls, rs, left_parity, right_parity, block, right_ops[0])
        sums.append(summed_over_ops(keep, give))
    row_parity = lax.dynamic_slice_in_dim(left_parity, sec, 1)
    out_parity = lax.dynamic_slice_in_dim(right_parity, ops * 2, 2)
    live = ((out_parity + row_parity) % 2 == 1)[:, None, None]
    result = jnp.concatenate([jnp.where(live, s, 0.0).astype(BF16) for s in sums], axis=1)
    return result[None]


def solution(mesh):
    placed = (
        P(None, "sec", None, None),
        P("ops", None, None, None),
        P("ops", None),
        P("ops", None, None, None),
        P("ops", None),
        P(),
        P(),
    )
    return jax.shard_map(
        local, mesh=mesh, in_specs=placed, out_specs=P("sec", "ops", None, None), check_vma=False
    )
```

time: 291 us -> 201 us (0.69); the launches traced: 290 us -> 203 us
  waiting for transfers between devices: 200 us -> 68.3 us
  blocking collectives: 0 us -> 70.3 us
  Pallas kernels: 0 us -> 23.4 us
  matrix products: 23.2 us -> 0 us
  local copies, waits for them, and re-layouts: 31.1 us -> 11.7 us
  between operations: 13.5 us -> 0.16 us
  starting transfers between devices: 8.82 us -> 19.4 us
  other arithmetic: 13.1 us -> 9.82 us
    all_to_all x1, waiting for transfers between devices: 146 us -> 28 us  [local(): block = lax.all_to_all(send, 'sec', 0, 0, tiled=True)]
    all_to_all x0 -> x1, blocking collectives: none -> 70.3 us  [local(): block = lax.all_to_all(send, 'sec', 0, 0, tiled=True)]
    reduce_scatter x1 -> x0, waiting for transfers between devices: 54.5 us -> none  [local(): lax.psum_scatter(jnp.einsum('gikab,gkcb->kiac', picked, right_ops, prefer...]
    ppermute x0 -> x8, waiting for transfers between devices: none -> 40.3 us  [the longest x6 37 us: summed_over_ops(): part = lax.ppermute(part, 'ops', [(o, (o + 2 * hop) % n) for o in range(n)])]
    pallas_call x0 -> x3, Pallas kernels: none -> 23.4 us  [the longest x2 14.4 us: right_products(): pl.pallas_call(right_kernel, out_shape=[half, half], in_specs=[smem] * 5...]
    dot_general x2 -> x0, matrix products: 23.2 us -> none  [the longest x1 11.8 us: local(): jnp.einsum('giab,gikbc->gikac', left_ops, source_rows, preferred_element_...]
    gather x3 -> x0, local copies, waits for them, and re-layouts: 16.3 us -> none  [the longest x2 8.17 us: take_columns(): return jnp.take(column_block, column_index, axis=1)]
    ppermute x0 -> x8, starting transfers between devices: none -> 15 us  [the longest x6 8.99 us: summed_over_ops(): part = lax.ppermute(part, 'ops', [(o, (o + 2 * hop) % n) for o in range(n)])]
  transfers between devices with their start and end apart: 2 -> 9, of which waited for: 2 -> 6; matrix products, arithmetic and copies ran while one was open for 0% -> 5% of each run, Pallas kernels for 0% -> 7%
where the time goes in v1:
time: 201 us; the launch traced here: 203 us
  blocking collectives  70.3 us (35%)
  waiting for transfers between devices  68.3 us (34%)
  Pallas kernels  23.4 us (12%)
  starting transfers between devices  19.4 us (10%)
  local copies, waits for them, and re-layouts  11.7 us (6%)
  other arithmetic  9.82 us (5%)
    all_to_all x1, blocking collectives, local(): block = lax.all_to_all(send, 'sec', 0, 0, tiled=True)  70.3 us
    ppermute x6, waiting for transfers between devices, summed_over_ops(): part = lax.ppermute(part, 'ops', [(o, (o + 2 * hop) % n) for o in range(n)])  37 us
    all_to_all x1, waiting for transfers between devices, local(): block = lax.all_to_all(send, 'sec', 0, 0, tiled=True)  28 us
    pallas_call x2, Pallas kernels, right_products(): pl.pallas_call(right_kernel, out_shape=[half, half], in_specs=[smem] * 5...  14.4 us
    ppermute x6, starting transfers between devices, summed_over_ops(): part = lax.ppermute(part, 'ops', [(o, (o + 2 * hop) % n) for o in range(n)])  8.99 us
    pallas_call x1, Pallas kernels, left_products(): pl.pallas_call(left_kernel, out_shape=[jax.ShapeDtypeStruct((k, rows, m),...  8.96 us
    unnamed x30, local copies, waits for them, and re-layouts  8.67 us
    ppermute x2, starting transfers between devices, summed_over_ops(): got = lax.ppermute(give, 'ops', [(o, o ^ 1) for o in range(n)])  6 us
  transfers between devices with their start and end apart: 9, of which 6 were waited for; matrix products, arithmetic and copies ran while one was open for 5% of the time, Pallas kernels for 7%

profile of v1, /device:TPU:1, one launch (start us, length us, event | category | flops | bytes accessed | tf_op | source)
XLA Modules:
  0.0 203.0 jit_solution(16727264683659549490)
XLA Ops:
  0.0 0.1 pad_add_fusion.me
  0.1 0.0 copy-start.5
  0.1 0.7 copy-done.5
  0.7 0.0 copy-start.7
  0.7 0.7 copy-done.7
  1.4 0.0 copy-start.9
  1.4 0.7 copy-done.9
  2.0 0.0 copy-start.11
  2.0 0.7 copy-done.11
  2.7 9.0 %left_products.1 = (bf16[16,320,512]{2,1,0:T(8,128)(2,1)S(1)}, bf16[16,192,512]{2,1,0:T(8,128)(2,1)S(1)}) custom-call(s32[2]{0:T(128)S(1)} %pad_add_fusion.me, s32[16]{0:T(128)S(1)} %bitcast.10, s32[16]{0:T(128)S(1)} %bitcast.13, s32[16]{0:T(128)S(1)} %copy-done.11, s32[16]{0:T(128)S(1)} %copy-done.5, bf16[16,512,512]{2,1,0:T(8,128)(2,1)} %bitcast.18, ...), custom_call_target="tpu_custom_call" | custom-call | flops 1073741824 | bytes 6291456 | tf_op jit(solution)/shard_map/left_products/pallas_call | solution.py:73
  11.7 0.0 copy-start.1
  11.7 70.3 %all_to_all.10.block = bf16[16,320,512]{2,1,0:T(8,128)(2,1)} all-to-all(bf16[16,320,512]{2,1,0:T(8,128)(2,1)S(1)} %get-tuple-element.11), channel_id=1, replica_groups=mesh['ops'=8,'sec'=16] {'sec'}, dimensions={0} | all-to-all | bytes 10485760 | tf_op jit(solution)/shard_map/all_to_all | solution.py:218
  82.0 0.0 copy-done.1
  82.0 0.0 copy-start.6
  82.0 0.0 copy-start.8
  82.0 0.0 copy-start.10
  82.0 0.0 copy-start.12
  82.0 4.4 %all-to-all-start.1 = ((bf16[16,192,512]{2,1,0:T(8,128)(2,1)}), bf16[16,192,512]{2,1,0:T(8,128)(2,1)S(1)}, u32[]{:S(2)}, u32[]{:S(2)}) async-start(bf16[16,192,512]{2,1,0:T(8,128)(2,1)} %copy-done.1), calls=%async_computation.1 | async-start | bytes 6291456 | tf_op jit(solution)/shard_map/all_to_all | solution.py:218
  86.4 0.0 copy-done.6
  86.4 0.0 copy-done.8
  86.4 0.0 copy-done.10
  86.4 0.0 copy-done.12
  86.4 0.0 copy-start
  86.4 2.5 %copy-done = bf16[16,320,512]{2,1,0:T(8,128)(2,1)S(1)} copy-done((bf16[16,320,512]{2,1,0:T(8,128)(2,1)S(1)}, bf16[16,320,512]{2,1,0:T(8,128)(2,1)}, u32[]{:S(2)}) %copy-start) | copy-done | bytes 5242904
  88.9 6.5 %right_products.2 = (bf16[8,320,512]{2,1,0:T(8,128)(2,1)S(1)}, bf16[8,320,512]{2,1,0:T(8,128)(2,1)}) custom-call(s32[2]{0:T(128)S(1)} %pad_add_fusion.me, s32[16]{0:T(128)S(1)} %bitcast.11, s32[16]{0:T(128)S(1)} %bitcast.14, s32[16]{0:T(128)S(1)} %copy-done.12, s32[16]{0:T(128)S(1)} %copy-done.6, bf16[16,320,512]{2,1,0:T(8,128)(2,1)S(1)} %copy-done, ...), custom_call_target="tpu_custom_call" | custom-call | flops 1342177280 | bytes 9437184 | tf_op jit(solution)/shard_map/right_products/pallas_call | solution.py:174
  95.4 0.0 copy-start.2
  95.4 1.5 copy-done.2
  97.0 1.8 collective-permute-start
  98.8 28.0 %all-to-all-done.1.block = bf16[16,192,512]{2,1,0:T(8,128)(2,1)S(1)} async-done(((bf16[16,192,512]{2,1,0:T(8,128)(2,1)}), bf16[16,192,512]{2,1,0:T(8,128)(2,1)S(1)}, u32[]{:S(2)}, u32[]{:S(2)}) %all-to-all-start.1) | async-done | bytes 3145760 | tf_op jit(solution)/shard_map/all_to_all | solution.py:218
  126.8 7.9 %right_products.3 = (bf16[8,192,512]{2,1,0:T(8,128)(2,1)S(1)}, bf16[8,192,512]{2,1,0:T(8,128)(2,1)}) custom-call(s32[2]{0:T(128)S(1)} %pad_add_fusion.me, s32[16]{0:T(128)S(1)} %bitcast.12, s32[16]{0:T(128)S(1)} %bitcast.15, s32[16]{0:T(128)S(1)} %copy-done.12, s32[16]{0:T(128)S(1)} %copy-done.6, bf16[16,192,512]{2,1,0:T(8,128)(2,1)S(1)} %all-to-all-done.1.block, ...), custom_call_target="tpu_custom_call" | custom-call | flops 805306368 | bytes 7340032 | tf_op jit(solution)/shard_map/right_products/pallas_call | solution.py:174
  134.7 0.0 copy-start.4
  134.7 1.2 copy-done.4
  136.0 4.2 %collective-permute-start.4 = (bf16[8,192,512]{2,1,0:T(8,128)(2,1)}, bf16[8,192,512]{2,1,0:T(8,128)(2,1)S(1)}, u32[]{:S(2)}, u32[]{:S(2)}) collective-permute-start(bf16[8,192,512]{2,1,0:T(8,128)(2,1)} %get-tuple-element.16), channel_id=1, source_target_pairs={{0,16},{16,0},{32,48},{48,32},{64,80},{80,64},{96,112},{112,96},{1... | collective-permute-start | bytes 4718600 | tf_op jit(solution)/shard_map/ppermute | solution.py:200
  140.2 3.2 %collective-permute-done.4 = bf16[8,192,512]{2,1,0:T(8,128)(2,1)S(1)} collective-permute-done((bf16[8,192,512]{2,1,0:T(8,128)(2,1)}, bf16[8,192,512]{2,1,0:T(8,128)(2,1)S(1)}, u32[]{:S(2)}, u32[]{:S(2)}) %collective-permute-start.4) | collective-permute-done | bytes 1572896 | tf_op jit(solution)/shard_map/ppermute | solution.py:200
  143.4 0.0 copy-start.3
  143.4 2.0 add_convert_fusion.1
  145.4 0.0 copy-start.13
  145.5 1.2 constant_dynamic-slice_fusion.2
  146.6 4.6 %collective-permute-start.7 = (bf16[2,192,512]{2,1,0:T(8,128)(2,1)S(1)}, bf16[2,192,512]{2,1,0:T(8,128)(2,1)S(1)}, u32[]{:S(2)}, u32[]{:S(2)}) collective-permute-start(bf16[2,192,512]{2,1,0:T(8,128)(2,1)S(1)} %get-tuple-element.21), channel_id=1, source_target_pairs={{0,96},{16,112},{32,0},{48,16},{64,32},{80,48},{96,64},{112,80},{1... | collective-permute-start | bytes 1179656 | tf_op jit(solution)/shard_map/ppermute | solution.py:206
  151.2 0.0 collective-permute-start.6
  151.2 0.6 collective-permute-start.5
  151.7 0.0 collective-permute-done
  151.7 0.0 copy-done.13
  151.8 0.0 copy-done.3
  151.8 2.5 %add_convert_fusion = bf16[8,320,512]{2,1,0:T(8,128)(2,1)S(1)} fusion(bf16[8,320,512]{2,1,0:T(8,128)(2,1)} %collective-permute-done, bf16[8,320,512]{2,1,0:T(8,128)(2,1)S(1)} %copy-done.3), kind=kLoop, calls=%fused_computation | loop fusion | flops 5242880 | bytes 7864320 | tf_op jit(solution)/shard_map/convert_element_type | solution.py:201
  154.3 1.2 constant_dynamic-slice_fusion.5
  155.5 2.1 %collective-permute-start.3 = (bf16[2,320,512]{2,1,0:T(8,128)(2,1)}, bf16[2,320,512]{2,1,0:T(8,128)(2,1)}, u32[]{:S(2)}, u32[]{:S(2)}) collective-permute-start(bf16[2,320,512]{2,1,0:T(8,128)(2,1)} %get-tuple-element.18), channel_id=1, source_target_pairs={{0,96},{16,112},{32,0},{48,16},{64,32},{80,48},{96,64},{112,80},{1... | collective-permute-start | bytes 1966088 | tf_op jit(solution)/shard_map/ppermute | solution.py:206
  157.6 1.8 collective-permute-start.2
  159.4 8.3 %collective-permute-done.7 = bf16[2,192,512]{2,1,0:T(8,128)(2,1)S(1)} collective-permute-done((bf16[2,192,512]{2,1,0:T(8,128)(2,1)S(1)}, bf16[2,192,512]{2,1,0:T(8,128)(2,1)S(1)}, u32[]{:S(2)}, u32[]{:S(2)}) %collective-permute-start.7) | collective-permute-done | bytes 393248 | tf_op jit(solution)/shard_map/ppermute | solution.py:206
  167.7 0.0 copy-start.14
  167.7 0.8 copy-done.14
  168.5 0.0 collective-permute-start.1
  168.5 0.6 dynamic_slice.31
  169.1 0.7 fusion
  169.8 0.0 collective-permute-done.6
  169.9 2.3 %collective-permute-done.5 = bf16[2,192,512]{2,1,0:T(8,128)(2,1)} collective-permute-done((bf16[2,192,512]{2,1,0:T(8,128)(2,1)}, bf16[2,192,512]{2,1,0:T(8,128)(2,1)}, u32[]{:S(2)}, u32[]{:S(2)}) %collective-permute-start.5) | collective-permute-done | bytes 393248 | tf_op jit(solution)/shard_map/ppermute | solution.py:206
  172.2 1.6 select_convert_fusion.1
  173.8 22.1 %collective-permute-done.3 = bf16[2,320,512]{2,1,0:T(8,128)(2,1)} collective-permute-done((bf16[2,320,512]{2,1,0:T(8,128)(2,1)}, bf16[2,320,512]{2,1,0:T(8,128)(2,1)}, u32[]{:S(2)}, u32[]{:S(2)}) %collective-permute-start.3) | collective-permute-done | bytes 655392 | tf_op jit(solution)/shard_map/ppermute | solution.py:206
  195.9 0.0 collective-permute-done.2
  195.9 4.2 %collective-permute-done.1 = bf16[2,320,512]{2,1,0:T(8,128)(2,1)} collective-permute-done((bf16[2,320,512]{2,1,0:T(8,128)(2,1)S(1)}, bf16[2,320,512]{2,1,0:T(8,128)(2,1)}, u32[]{:S(2)}, u32[]{:S(2)}) %collective-permute-start.1) | collective-permute-done | bytes 655392 | tf_op jit(solution)/shard_map/ppermute | solution.py:206
  200.1 1.9 select_convert_fusion
  202.0 1.0 maximum_bitcast_fusion
Async XLA Ops:
  0.1 0.7 copy-start.5
  0.7 0.7 copy-start.7
  1.4 0.7 copy-start.9
  2.0 0.7 copy-start.11
  11.7 70.3 %copy-start.1 = (bf16[16,192,512]{2,1,0:T(8,128)(2,1)}, bf16[16,192,512]{2,1,0:T(8,128)(2,1)S(1)}, u32[]{:S(2)}) copy-start(bf16[16,192,512]{2,1,0:T(8,128)(2,1)S(1)} %get-tuple-element.14) | copy-start | bytes 9437188
  82.0 4.4 %copy-start.6 = (s32[16]{0:T(128)S(1)}, s32[16]{0:T(128)}, u32[]{:S(2)}) copy-start(s32[16]{0:T(128)} %rp.5) | copy-start | bytes 196
  82.0 4.4 %copy-start.8 = (s32[1,16]{1,0:T(1,128)S(1)}, s32[1,16]{1,0:T(1,128)}, u32[]{:S(2)}) copy-start(s32[1,16]{1,0:T(1,128)} %param.9) | copy-start | bytes 196
  82.0 4.4 %copy-start.10 = (s32[1,16]{1,0:T(1,128)S(1)}, s32[1,16]{1,0:T(1,128)}, u32[]{:S(2)}) copy-start(s32[1,16]{1,0:T(1,128)} %param.11) | copy-start | bytes 196
  82.0 4.4 %copy-start.12 = (s32[16]{0:T(128)S(1)}, s32[16]{0:T(128)}, u32[]{:S(2)}) copy-start(s32[16]{0:T(128)} %lp.5) | copy-start | bytes 196
  82.0 44.8 %all-to-all-start.1 = ((bf16[16,192,512]{2,1,0:T(8,128)(2,1)}), bf16[16,192,512]{2,1,0:T(8,128)(2,1)S(1)}, u32[]{:S(2)}, u32[]{:S(2)}) async-start(bf16[16,192,512]{2,1,0:T(8,128)(2,1)} %copy-done.1), calls=%async_computation.1 | async-start | bytes 6291456 | tf_op jit(solution)/shard_map/all_to_all | solution.py:218
  86.4 2.5 %copy-start = (bf16[16,320,512]{2,1,0:T(8,128)(2,1)S(1)}, bf16[16,320,512]{2,1,0:T(8,128)(2,1)}, u32[]{:S(2)}) copy-start(bf16[16,320,512]{2,1,0:T(8,128)(2,1)} %all_to_all.10.block) | copy-start | bytes 15728644
  95.4 1.6 copy-start.2
  97.0 54.8 %collective-permute-start = (bf16[8,320,512]{2,1,0:T(8,128)(2,1)}, bf16[8,320,512]{2,1,0:T(8,128)(2,1)}, u32[]{:S(2)}, u32[]{:S(2)}) collective-permute-start(bf16[8,320,512]{2,1,0:T(8,128)(2,1)} %get-tuple-element.13), channel_id=1, source_target_pairs={{0,16},{16,0},{32,48},{48,32},{64,80},{80,64},{96,112},{112,96},{1... | collective-permute-start | bytes 7864328 | tf_op jit(solution)/shard_map/ppermute | solution.py:200
  134.7 1.2 copy-start.4
  136.0 7.5 %collective-permute-start.4 = (bf16[8,192,512]{2,1,0:T(8,128)(2,1)}, bf16[8,192,512]{2,1,0:T(8,128)(2,1)S(1)}, u32[]{:S(2)}, u32[]{:S(2)}) collective-permute-start(bf16[8,192,512]{2,1,0:T(8,128)(2,1)} %get-tuple-element.16), channel_id=1, source_target_pairs={{0,16},{16,0},{32,48},{48,32},{64,80},{80,64},{96,112},{112,96},{1... | collective-permute-start | bytes 4718600 | tf_op jit(solution)/shard_map/ppermute | solution.py:200
  143.4 8.3 %copy-start.3 = (bf16[8,320,512]{2,1,0:T(8,128)(2,1)S(1)}, bf16[8,320,512]{2,1,0:T(8,128)(2,1)}, u32[]{:S(2)}) copy-start(bf16[8,320,512]{2,1,0:T(8,128)(2,1)} %copy-done.2) | copy-start | bytes 7864324
  145.4 6.3 %copy-start.13 = (bf16[8,192,512]{2,1,0:T(8,128)(2,1)}, bf16[8,192,512]{2,1,0:T(8,128)(2,1)S(1)}, u32[]{:S(2)}) copy-start(bf16[8,192,512]{2,1,0:T(8,128)(2,1)S(1)} %add_convert_fusion.1) | copy-start | bytes 4718596
  146.6 21.1 %collective-permute-start.7 = (bf16[2,192,512]{2,1,0:T(8,128)(2,1)S(1)}, bf16[2,192,512]{2,1,0:T(8,128)(2,1)S(1)}, u32[]{:S(2)}, u32[]{:S(2)}) collective-permute-start(bf16[2,192,512]{2,1,0:T(8,128)(2,1)S(1)} %get-tuple-element.21), channel_id=1, source_target_pairs={{0,96},{16,112},{32,0},{48,16},{64,32},{80,48},{96,64},{112,80},{1... | collective-permute-start | bytes 1179656 | tf_op jit(solution)/shard_map/ppermute | solution.py:206
  151.2 18.7 %collective-permute-start.6 = (bf16[2,192,512]{2,1,0:T(8,128)(2,1)}, bf16[2,192,512]{2,1,0:T(8,128)(2,1)}, u32[]{:S(2)}, u32[]{:S(2)}) collective-permute-start(bf16[2,192,512]{2,1,0:T(8,128)(2,1)} %get-tuple-element.22), channel_id=1, source_target_pairs={{0,64},{16,80},{32,96},{48,112},{64,0},{80,16},{96,32},{112,48},{1... | collective-permute-start | bytes 1179656 | tf_op jit(solution)/shard_map/ppermute | solution.py:206
  151.2 21.0 %collective-permute-start.5 = (bf16[2,192,512]{2,1,0:T(8,128)(2,1)}, bf16[2,192,512]{2,1,0:T(8,128)(2,1)}, u32[]{:S(2)}, u32[]{:S(2)}) collective-permute-start(bf16[2,192,512]{2,1,0:T(8,128)(2,1)} %get-tuple-element.20), channel_id=1, source_target_pairs={{0,32},{16,48},{32,64},{48,80},{64,96},{80,112},{96,0},{112,16},{1... | collective-permute-start | bytes 1179656 | tf_op jit(solution)/shard_map/ppermute | solution.py:206
  155.5 40.4 %collective-permute-start.3 = (bf16[2,320,512]{2,1,0:T(8,128)(2,1)}, bf16[2,320,512]{2,1,0:T(8,128)(2,1)}, u32[]{:S(2)}, u32[]{:S(2)}) collective-permute-start(bf16[2,320,512]{2,1,0:T(8,128)(2,1)} %get-tuple-element.18), channel_id=1, source_target_pairs={{0,96},{16,112},{32,0},{48,16},{64,32},{80,48},{96,64},{112,80},{1... | collective-permute-start | bytes 1966088 | tf_op jit(solution)/shard_map/ppermute | solution.py:206
  157.6 38.3 %collective-permute-start.2 = (bf16[2,320,512]{2,1,0:T(8,128)(2,1)}, bf16[2,320,512]{2,1,0:T(8,128)(2,1)}, u32[]{:S(2)}, u32[]{:S(2)}) collective-permute-start(bf16[2,320,512]{2,1,0:T(8,128)(2,1)} %get-tuple-element.19), channel_id=1, source_target_pairs={{0,64},{16,80},{32,96},{48,112},{64,0},{80,16},{96,32},{112,48},{1... | collective-permute-start | bytes 1966088 | tf_op jit(solution)/shard_map/ppermute | solution.py:206
  167.7 0.8 copy-start.14
  168.5 31.7 %collective-permute-start.1 = (bf16[2,320,512]{2,1,0:T(8,128)(2,1)S(1)}, bf16[2,320,512]{2,1,0:T(8,128)(2,1)}, u32[]{:S(2)}, u32[]{:S(2)}) collective-permute-start(bf16[2,320,512]{2,1,0:T(8,128)(2,1)S(1)} %get-tuple-element.17), channel_id=1, source_target_pairs={{0,32},{16,48},{32,64},{48,80},{64,96},{80,112},{96,0},{112,16},{1... | collective-permute-start | bytes 1966088 | tf_op jit(solution)/shard_map/ppermute | solution.py:206

commit v2 on v1

v2 whole, which is shorter than its diff:
```python
import functools

import jax
import jax.numpy as jnp
from jax import lax
from jax.experimental import pallas as pl
from jax.experimental.pallas import tpu as pltpu
from jax.sharding import PartitionSpec as P

CHUNKS = (320, 192)
F32 = jnp.float32
BF16 = jnp.bfloat16
MIB = 1024 * 1024
HBM = pl.BlockSpec(memory_space=pl.ANY)


def read_lists(given, held, sem):
    copies = [pltpu.make_async_copy(g, h, sem.at[n]) for n, (g, h) in enumerate(zip(given, held))]
    for copy in copies:
        copy.start()
    for copy in copies:
        copy.wait()


def list_scratch(k):
    return [pltpu.SMEM((k,), jnp.int32)] * 4 + [pltpu.SemaphoreType.DMA((4,))]


def left_kernel(*refs):
    lists, (psi, left), outs = refs[:4], refs[4:6], refs[6 : 6 + len(CHUNKS)]
    held, list_sem, items, pbuf, lbuf, obuf, psem, lsem, osem = refs[6 + len(CHUNKS):][:4], *refs[10 + len(CHUNKS):]
    read_lists(lists, held, list_sem)
    ls, rs, lp, rp = held
    sectors = psi.shape[0]
    col = lax.axis_index("sec")
    col_parity = rp[col] & 1

    def scan(k, flags):
        hit = (rs[k] == col).astype(jnp.int32)
        odd = rp[k] & 1
        return flags[0] | (hit * odd), flags[1] | (hit * (1 - odd))

    for_even, for_odd = lax.fori_loop(0, sectors, scan, (jnp.int32(0), jnp.int32(0)))

    def fetch(i, count):
        source = ls[i]
        wanted = jnp.where((lp[i] & 1) == 1, for_odd, for_even)
        need = (wanted == 1) & ((lp[source] & 1) != col_parity)

        @pl.when(need)
        def _():
            items[count] = i
            pltpu.make_async_copy(psi.at[source], pbuf.at[count], psem.at[count]).start()
            pltpu.make_async_copy(left.at[i], lbuf.at[count], lsem.at[count]).start()

        return count + need.astype(jnp.int32)

    count = lax.fori_loop(0, sectors, fetch, jnp.int32(0))

    def stores(j):
        at = 0
        for c, rows in enumerate(CHUNKS):
            yield pltpu.make_async_copy(
                obuf.at[j, pl.ds(at, rows)], outs[c].at[items[j]], osem.at[c, j]
            )
            at += rows

    def work(j, carry):
        pltpu.make_async_copy(psi.at[0], pbuf.at[j], psem.at[j]).wait()
        pltpu.make_async_copy(left.at[0], lbuf.at[j], lsem.at[j]).wait()
        obuf[j] = jnp.dot(lbuf[j], pbuf[j], preferred_element_type=F32).astype(BF16)
        for copy in stores(j):
            copy.start()
        return carry

    lax.fori_loop(0, count, work, 0)

    def finish(j, carry):
        for copy in stores(j):
            copy.wait()
        return carry

    lax.fori_loop(0, count, finish, 0)


def left_products(lists, psi, left):
    k, m = psi.shape[0], psi.shape[-1]
    return pl.pallas_call(
        left_kernel,
        out_shape=[jax.ShapeDtypeStruct((k, rows, m), BF16) for rows in CHUNKS],
        in_specs=[HBM] * 6,
        out_specs=[HBM] * len(CHUNKS),
        scratch_shapes=list_scratch(k) + [
            pltpu.SMEM((k,), jnp.int32),
            pltpu.VMEM((k, m, m), BF16),
            pltpu.VMEM((k, m, m), BF16),
            pltpu.VMEM((k, m, m), BF16),
            pltpu.SemaphoreType.DMA((k,)),
            pltpu.SemaphoreType.DMA((k,)),
            pltpu.SemaphoreType.DMA((len(CHUNKS), k)),
        ],
        compiler_params=pltpu.CompilerParams(vmem_limit_bytes=56 * MIB),
        cost_estimate=pl.CostEstimate(
            flops=8 * m ** 3, bytes_accessed=12 * m * m * 2, transcendentals=0
        ),
        name="left_products",
    )(*lists, psi, left)


def right_kernel(first, *refs):
    lists, (block, right, keep, give), refs = refs[:4], refs[4:8], refs[8:]
    if first:
        turned, refs = refs[0], refs[1:]
    held, (list_sem, items, zbuf, sbuf, rbuf, obuf, ssem, rsem, osem), refs = refs[:4], refs[4:13], refs[13:]
    if first:
        tbuf, tsem = refs
    read_lists(lists, held, list_sem)
    ls, rs, lp, rp = held
    sectors = right.shape[0]
    row, core = lax.axis_index("sec"), lax.axis_index("ops") % 2
    row_parity = lp[row] & 1
    source_parity = lp[ls[row]] & 1
    zbuf[...] = jnp.zeros_like(zbuf)

    def place(buf, k):
        slot = (k // 4) * 2 + k % 2
        mine = (k // 2) % 2 == core

        @pl.when(mine)
        def _():
            pltpu.make_async_copy(buf, keep.at[slot], osem.at[k]).start()

        @pl.when(jnp.logical_not(mine))
        def _():
            pltpu.make_async_copy(buf, give.at[slot], osem.at[k]).start()

    def fetch(k, count):
        live = (rp[k] & 1) != row_parity
        source = rs[k]
        need = live & ((rp[source] & 1) != source_parity)

        @pl.when(need)
        def _():
            items[count] = k
            pltpu.make_async_copy(block.at[source], sbuf.at[count], ssem.at[count]).start()
            pltpu.make_async_copy(right.at[k], rbuf.at[count], rsem.at[count]).start()

        @pl.when(live & jnp.logical_not(need))
        def _():
            place(zbuf, k)

        return count + need.astype(jnp.int32)

    count = lax.fori_loop(0, sectors, fetch, jnp.int32(0))

    def work(j, carry):
        pltpu.make_async_copy(right.at[0], rbuf.at[j], rsem.at[j]).wait()
        if first:
            tbuf[j] = rbuf[j].T
            pltpu.make_async_copy(tbuf.at[j], turned.at[items[j]], tsem.at[j]).start()
        pltpu.make_async_copy(block.at[0], sbuf.at[j], ssem.at[j]).wait()
        factor = tbuf[j] if first else rbuf[j]
        obuf[j] = jnp.dot(sbuf[j], factor, preferred_element_type=F32).astype(BF16)
        place(obuf.at[j], items[j])
        return carry

    lax.fori_loop(0, count, work, 0)

    def finish(k, carry):
        @pl.when((rp[k] & 1) != row_parity)
        def _():
            pltpu.make_async_copy(zbuf, keep.at[0], osem.at[k]).wait()

        return carry

    lax.fori_loop(0, sectors, finish, 0)
    if first:
        def turn(j, carry):
            pltpu.make_async_copy(tbuf.at[j], turned.at[0], tsem.at[j]).wait()
            return carry

        lax.fori_loop(0, count, turn, 0)


def right_products(lists, block, right, first):
    k, rows, m = block.shape
    out = [jax.ShapeDtypeStruct((k // 2, rows, m), BF16)] * 2
    extra = []
    if first:
        out = out + [jax.ShapeDtypeStruct((k, m, m), BF16)]
        extra = [pltpu.VMEM((k, m, m), BF16), pltpu.SemaphoreType.DMA((k,))]
    return pl.pallas_call(
        functools.partial(right_kernel, first),
        out_shape=out,
        in_specs=[HBM] * 6,
        out_specs=[HBM] * len(out),
        scratch_shapes=list_scratch(k) + [
            pltpu.SMEM((k,), jnp.int32),
            pltpu.VMEM((rows, m), BF16),
            pltpu.VMEM((k, rows, m), BF16),
            pltpu.VMEM((k, m, m), BF16),
            pltpu.VMEM((k, rows, m), BF16),
            pltpu.SemaphoreType.DMA((k,)),
            pltpu.SemaphoreType.DMA((k,)),
            pltpu.SemaphoreType.DMA((k,)),
        ] + extra,
        compiler_params=pltpu.CompilerParams(vmem_limit_bytes=56 * MIB),
        cost_estimate=pl.CostEstimate(
            flops=16 * rows * m * m, bytes_accessed=8 * m * m * 2 + 16 * rows * m * 2, transcendentals=0
        ),
        name="right_products",
    )(*lists, block, right)


def summed_over_ops(keep, give):
    n = 8
    got = lax.ppermute(give, "ops", [(o, o ^ 1) for o in range(n)])
    pair = (keep.astype(F32) + got.astype(F32)).astype(BF16)
    chip = lax.axis_index("ops") // 2
    total = lax.dynamic_slice_in_dim(pair, chip * 2, 2).astype(F32)
    for hop in (1, 2, 3):
        part = lax.dynamic_slice_in_dim(pair, (chip + hop) % 4 * 2, 2)
        part = lax.ppermute(part, "ops", [(o, (o + 2 * hop) % n) for o in range(n)])
        total = total + part.astype(F32)
    return total


def local(psi, left_ops, left_src, right_ops, right_src, left_parity, right_parity):
    sec, ops = lax.axis_index("sec"), lax.axis_index("ops")
    lists = (left_src[0], right_src[0], left_parity, right_parity)
    row_parity = lax.dynamic_slice_in_dim(left_parity, sec, 1)
    out_parity = lax.dynamic_slice_in_dim(right_parity, ops * 2, 2)
    live = ((out_parity + row_parity) % 2 == 1)[:, None, None]
    sends = left_products(lists, psi[:, 0], left_ops[0])
    blocks = [lax.all_to_all(send, "sec", 0, 0, tiled=True) for send in sends]
    keep, give, turned = right_products(lists, blocks[0], right_ops[0], True)
    early = jnp.where(live, summed_over_ops(keep, give), 0.0).astype(BF16)
    early, last = lax.optimization_barrier((early, blocks[1]))
    keep, give = right_products(lists, last, turned, False)
    late = jnp.where(live, summed_over_ops(keep, give), 0.0).astype(BF16)
    return jnp.concatenate([early, late], axis=1)[None]


def solution(mesh):
    placed = (
        P(None, "sec", None, None),
        P("ops", None, None, None),
        P("ops", None),
        P("ops", None, None, None),
        P("ops", None),
        P(),
        P(),
    )
    return jax.shard_map(
        local, mesh=mesh, in_specs=placed, out_specs=P("sec", "ops", None, None), check_vma=False
    )
```

time: 201 us -> 174 us (0.87); the launches traced: 203 us -> 171 us
  waiting for transfers between devices: 68.3 us -> 52.7 us
  Pallas kernels: 23.4 us -> 15.2 us
  local copies, waits for them, and re-layouts: 11.7 us -> 5.26 us
    all_to_all x1, waiting for transfers between devices: 28 us -> 0.01 us  [local(): blocks = [lax.all_to_all(send, 'sec', 0, 0, tiled=True) for send in sends]]
    ppermute x6, waiting for transfers between devices: 37 us -> 49.5 us  [summed_over_ops(): part = lax.ppermute(part, 'ops', [(o, (o + 2 * hop) % n) for o in range(n)])]
    pallas_call x2, Pallas kernels: 14.4 us -> 8.19 us  [right_products(): pl.pallas_call(functools.partial(right_kernel, first), out_shape=out, in_...]
    ppermute x6, starting transfers between devices: 8.99 us -> 3 us  [summed_over_ops(): part = lax.ppermute(part, 'ops', [(o, (o + 2 * hop) % n) for o in range(n)])]
    all_to_all x1, starting transfers between devices: 4.39 us -> 10.1 us  [local(): blocks = [lax.all_to_all(send, 'sec', 0, 0, tiled=True) for send in sends]]
    unnamed x30 -> x10, local copies, waits for them, and re-layouts: 8.67 us -> 3.29 us
  transfers between devices with their start and end apart: 9 -> 9, of which waited for: 6 -> 7; matrix products, arithmetic and copies ran while one was open for 5% -> 5% of each run, Pallas kernels for 7% -> 0%
where the time goes in v2:
time: 174 us; the launch traced here: 171 us
  blocking collectives  68.6 us (39%)
  waiting for transfers between devices  52.7 us (30%)
  starting transfers between devices  19 us (11%)
  Pallas kernels  15.2 us (9%)
  other arithmetic  9.97 us (6%)
  local copies, waits for them, and re-layouts  5.26 us (3%)
    all_to_all x1, blocking collectives, local(): blocks = [lax.all_to_all(send, 'sec', 0, 0, tiled=True) for send in sends]  68.6 us
    ppermute x6, waiting for transfers between devices, summed_over_ops(): part = lax.ppermute(part, 'ops', [(o, (o + 2 * hop) % n) for o in range(n)])  49.5 us
    all_to_all x1, starting transfers between devices, local(): blocks = [lax.all_to_all(send, 'sec', 0, 0, tiled=True) for send in sends]  10.1 us
    pallas_call x2, Pallas kernels, right_products(): pl.pallas_call(functools.partial(right_kernel, first), out_shape=out, in_...  8.19 us
    pallas_call x1, Pallas kernels, left_products(): pl.pallas_call(left_kernel, out_shape=[jax.ShapeDtypeStruct((k, rows, m),...  7.04 us
    ppermute x2, starting transfers between devices, summed_over_ops(): got = lax.ppermute(give, 'ops', [(o, o ^ 1) for o in range(n)])  5.88 us
    convert_element_type x2, other arithmetic, summed_over_ops(): pair = (keep.astype(F32) + got.astype(F32)).astype(BF16)  5.17 us
  transfers between devices with their start and end apart: 9, of which 7 were waited for; matrix products, arithmetic and copies ran while one was open for 5% of the time, Pallas kernels for 0%

profile of v2, /device:TPU:1, one launch (start us, length us, event | category | flops | bytes accessed | tf_op | source)
XLA Modules:
  0.0 171.0 jit_solution(11407174445201459583)
XLA Ops:
  0.0 7.0 %left_products.1 = (bf16[16,320,512]{2,1,0:T(8,128)(2,1)}, bf16[16,192,512]{2,1,0:T(8,128)(2,1)}) custom-call(s32[16]{0:T(128)} %bitcast.11, s32[16]{0:T(128)} %bitcast.14, s32[16]{0:T(128)} %refs_2_.5, s32[16]{0:T(128)} %refs_3_.5, bf16[16,512,512]{2,1,0:T(8,128)(2,1)} %bitcast.8, bf16[16,512,512]{2,1,0:T(8,128)(2,1)} %bitcast.9), custom_call_target="tpu_custom_call" | custom-call | flops 1073741824 | bytes 6291456 | tf_op jit(solution)/shard_map/left_products/pallas_call | solution.py:88
  7.1 68.6 %all_to_all.10.refs_4_ = bf16[16,320,512]{2,1,0:T(8,128)(2,1)} all-to-all(bf16[16,320,512]{2,1,0:T(8,128)(2,1)} %get-tuple-element.14), channel_id=1, replica_groups=mesh['ops'=8,'sec'=16] {'sec'}, dimensions={0} | all-to-all | bytes 10485760 | tf_op jit(solution)/shard_map/all_to_all | solution.py:235
  75.7 4.4 %right_products.2 = (bf16[8,320,512]{2,1,0:T(8,128)(2,1)}, bf16[8,320,512]{2,1,0:T(8,128)(2,1)}, bf16[16,512,512]{2,1,0:T(8,128)(2,1)}) custom-call(s32[16]{0:T(128)} %bitcast.12, s32[16]{0:T(128)} %bitcast.15, s32[16]{0:T(128)} %refs_2_.5, s32[16]{0:T(128)} %refs_3_.5, bf16[16,320,512]{2,1,0:T(8,128)(2,1)} %all_to_all.10.refs_4_, bf16[16,512,512]{2,1,0:T(8,128)(2,1)} %bitcast.10), custom_call_target="tpu_custom_call" | custom-call | flops 1342177280 | bytes 9437184 | tf_op jit(solution)/shard_map/right_products/pallas_call | solution.py:192
  80.1 4.0 %collective-permute-start = (bf16[8,320,512]{2,1,0:T(8,128)(2,1)}, bf16[8,320,512]{2,1,0:T(8,128)(2,1)}, u32[]{:S(2)}, u32[]{:S(2)}) collective-permute-start(bf16[8,320,512]{2,1,0:T(8,128)(2,1)} %get-tuple-element.16), channel_id=1, source_target_pairs={{0,16},{16,0},{32,48},{48,32},{64,80},{80,64},{96,112},{112,96},{1... | collective-permute-start | bytes 7864328 | tf_op jit(solution)/shard_map/ppermute | solution.py:217
  84.1 10.1 %all-to-all-start.1 = ((bf16[16,192,512]{2,1,0:T(8,128)(2,1)}), bf16[16,192,512]{2,1,0:T(8,128)(2,1)S(1)}, u32[]{:S(2)}, u32[]{:S(2)}) async-start(bf16[16,192,512]{2,1,0:T(8,128)(2,1)} %get-tuple-element.17), calls=%async_computation.1 | async-start | bytes 6291456 | tf_op jit(solution)/shard_map/all_to_all | solution.py:235
  94.2 0.0 collective-permute-done
  94.2 3.3 %add_convert_fusion = bf16[8,320,512]{2,1,0:T(8,128)(2,1)S(1)} fusion(bf16[8,320,512]{2,1,0:T(8,128)(2,1)} %collective-permute-done, bf16[8,320,512]{2,1,0:T(8,128)(2,1)} %get-tuple-element.15), kind=kLoop, calls=%fused_computation | loop fusion | flops 5242880 | bytes 7864320 | tf_op jit(solution)/shard_map/convert_element_type | solution.py:218
  97.5 0.0 copy-start.1
  97.6 1.6 copy-done.1
  99.1 0.0 copy-start.4
  99.1 0.0 copy-start.3
  99.1 1.3 constant_dynamic-slice_fusion.5
  100.4 0.0 collective-permute-start.3
  100.5 0.5 collective-permute-start.2
  100.9 1.0 collective-permute-start.1
  101.9 0.0 copy-done.4
  101.9 0.5 dynamic_slice.31
  102.5 0.0 copy-done.3
  102.5 0.6 fusion
  103.1 13.7 %collective-permute-done.3 = bf16[2,320,512]{2,1,0:T(8,128)(2,1)} collective-permute-done((bf16[2,320,512]{2,1,0:T(8,128)(2,1)}, bf16[2,320,512]{2,1,0:T(8,128)(2,1)}, u32[]{:S(2)}, u32[]{:S(2)}) %collective-permute-start.3) | collective-permute-done | bytes 655392 | tf_op jit(solution)/shard_map/ppermute | solution.py:223
  116.8 1.6 collective-permute-done.2
  118.3 14.6 %collective-permute-done.1 = bf16[2,320,512]{2,1,0:T(8,128)(2,1)} collective-permute-done((bf16[2,320,512]{2,1,0:T(8,128)(2,1)}, bf16[2,320,512]{2,1,0:T(8,128)(2,1)}, u32[]{:S(2)}, u32[]{:S(2)}) %collective-permute-start.1) | collective-permute-done | bytes 655392 | tf_op jit(solution)/shard_map/ppermute | solution.py:223
  133.0 2.9 %select_convert_fusion = bf16[2,320,512]{2,1,0:T(8,128)(2,1)} fusion(bf16[2,320,512]{2,1,0:T(8,128)(2,1)} %collective-permute-done.3, bf16[2,320,512]{2,1,0:T(8,128)(2,1)} %collective-permute-done.2, bf16[2,320,512]{2,1,0:T(8,128)(2,1)} %collective-permute-done.1, bf16[8,320,512]{2,1,0:T(8,128)(2,1)} %copy-done.1, s32[]{:T(128)S(6)} %select_n.66, ...), kind=kLoop, calls=%fused_computation.2 | loop fusion | flops 2949120 | bytes 3276806 | tf_op jit(solution)/shard_map/convert_element_type | solution.py:237
  135.9 0.0 all-to-all-done.1.refs_4_
  135.9 0.0 copy-start
  135.9 1.7 %copy-done = bf16[16,192,512]{2,1,0:T(8,128)(2,1)} copy-done((bf16[16,192,512]{2,1,0:T(8,128)(2,1)}, bf16[16,192,512]{2,1,0:T(8,128)(2,1)S(1)}, u32[]{:S(2)}) %copy-start) | copy-done | bytes 3145752
  137.6 3.8 %right_products.3 = (bf16[8,192,512]{2,1,0:T(8,128)(2,1)}, bf16[8,192,512]{2,1,0:T(8,128)(2,1)}) custom-call(s32[16]{0:T(128)} %bitcast.13, s32[16]{0:T(128)} %bitcast.16, s32[16]{0:T(128)} %refs_2_.5, s32[16]{0:T(128)} %refs_3_.5, bf16[16,192,512]{2,1,0:T(8,128)(2,1)} %copy-done, bf16[16,512,512]{2,1,0:T(8,128)(2,1)} %get-tuple-element.20.refs_5_), custom_call_target="tpu_custom_call" | custom-call | flops 805306368 | bytes 7340032 | tf_op jit(solution)/shard_map/right_products/pallas_call | solution.py:192
  141.4 1.9 %collective-permute-start.4 = (bf16[8,192,512]{2,1,0:T(8,128)(2,1)}, bf16[8,192,512]{2,1,0:T(8,128)(2,1)S(1)}, u32[]{:S(2)}, u32[]{:S(2)}) collective-permute-start(bf16[8,192,512]{2,1,0:T(8,128)(2,1)} %get-tuple-element.22), channel_id=1, source_target_pairs={{0,16},{16,0},{32,48},{48,32},{64,80},{80,64},{96,112},{112,96},{1... | collective-permute-start | bytes 4718600 | tf_op jit(solution)/shard_map/ppermute | solution.py:217
  143.3 3.2 %collective-permute-done.4 = bf16[8,192,512]{2,1,0:T(8,128)(2,1)S(1)} collective-permute-done((bf16[8,192,512]{2,1,0:T(8,128)(2,1)}, bf16[8,192,512]{2,1,0:T(8,128)(2,1)S(1)}, u32[]{:S(2)}, u32[]{:S(2)}) %collective-permute-start.4) | collective-permute-done | bytes 1572896 | tf_op jit(solution)/shard_map/ppermute | solution.py:217
  146.5 1.9 %add_convert_fusion.1 = bf16[8,192,512]{2,1,0:T(8,128)(2,1)S(1)} fusion(bf16[8,192,512]{2,1,0:T(8,128)(2,1)S(1)} %collective-permute-done.4, bf16[8,192,512]{2,1,0:T(8,128)(2,1)} %get-tuple-element.21), kind=kLoop, calls=%fused_computation.1 | loop fusion | flops 3145728 | bytes 4718592 | tf_op jit(solution)/shard_map/convert_element_type | solution.py:218
  148.4 0.0 copy-start.2
  148.4 0.1 constant_dynamic-slice_fusion.2
  148.5 0.1 collective-permute-start.7
  148.6 1.0 collective-permute-start.6
  149.6 0.5 collective-permute-start.5
  150.1 8.9 %collective-permute-done.7 = bf16[2,192,512]{2,1,0:T(8,128)(2,1)S(1)} collective-permute-done((bf16[2,192,512]{2,1,0:T(8,128)(2,1)S(1)}, bf16[2,192,512]{2,1,0:T(8,128)(2,1)S(1)}, u32[]{:S(2)}, u32[]{:S(2)}) %collective-permute-start.7) | collective-permute-done | bytes 393248 | tf_op jit(solution)/shard_map/ppermute | solution.py:223
  158.9 1.6 collective-permute-done.6
  160.6 9.1 %collective-permute-done.5 = bf16[2,192,512]{2,1,0:T(8,128)(2,1)S(1)} collective-permute-done((bf16[2,192,512]{2,1,0:T(8,128)(2,1)S(1)}, bf16[2,192,512]{2,1,0:T(8,128)(2,1)S(1)}, u32[]{:S(2)}, u32[]{:S(2)}) %collective-permute-start.5) | collective-permute-done | bytes 393248 | tf_op jit(solution)/shard_map/ppermute | solution.py:223
  169.7 0.2 select_convert_fusion.1
  169.9 0.0 copy-done.2
  169.9 1.0 maximum_bitcast_fusion
Async XLA Ops:
  80.1 14.1 %collective-permute-start = (bf16[8,320,512]{2,1,0:T(8,128)(2,1)}, bf16[8,320,512]{2,1,0:T(8,128)(2,1)}, u32[]{:S(2)}, u32[]{:S(2)}) collective-permute-start(bf16[8,320,512]{2,1,0:T(8,128)(2,1)} %get-tuple-element.16), channel_id=1, source_target_pairs={{0,16},{16,0},{32,48},{48,32},{64,80},{80,64},{96,112},{112,96},{1... | collective-permute-start | bytes 7864328 | tf_op jit(solution)/shard_map/ppermute | solution.py:217
  84.1 51.8 %all-to-all-start.1 = ((bf16[16,192,512]{2,1,0:T(8,128)(2,1)}), bf16[16,192,512]{2,1,0:T(8,128)(2,1)S(1)}, u32[]{:S(2)}, u32[]{:S(2)}) async-start(bf16[16,192,512]{2,1,0:T(8,128)(2,1)} %get-tuple-element.17), calls=%async_computation.1 | async-start | bytes 6291456 | tf_op jit(solution)/shard_map/all_to_all | solution.py:235
  97.5 1.6 copy-start.1
  99.1 2.8 %copy-start.4 = (s32[16]{0:T(128)S(1)}, s32[16]{0:T(128)}, u32[]{:S(2)}) copy-start(s32[16]{0:T(128)} %refs_2_.5) | copy-start | bytes 196
  99.1 3.4 %copy-start.3 = (s32[16]{0:T(128)S(1)}, s32[16]{0:T(128)}, u32[]{:S(2)}) copy-start(s32[16]{0:T(128)} %refs_3_.5) | copy-start | bytes 196
  100.4 16.3 %collective-permute-start.3 = (bf16[2,320,512]{2,1,0:T(8,128)(2,1)}, bf16[2,320,512]{2,1,0:T(8,128)(2,1)}, u32[]{:S(2)}, u32[]{:S(2)}) collective-permute-start(bf16[2,320,512]{2,1,0:T(8,128)(2,1)} %get-tuple-element.24), channel_id=1, source_target_pairs={{0,96},{16,112},{32,0},{48,16},{64,32},{80,48},{96,64},{112,80},{1... | collective-permute-start | bytes 1966088 | tf_op jit(solution)/shard_map/ppermute | solution.py:223
  100.5 17.9 %collective-permute-start.2 = (bf16[2,320,512]{2,1,0:T(8,128)(2,1)}, bf16[2,320,512]{2,1,0:T(8,128)(2,1)}, u32[]{:S(2)}, u32[]{:S(2)}) collective-permute-start(bf16[2,320,512]{2,1,0:T(8,128)(2,1)} %get-tuple-element.25), channel_id=1, source_target_pairs={{0,64},{16,80},{32,96},{48,112},{64,0},{80,16},{96,32},{112,48},{1... | collective-permute-start | bytes 1966088 | tf_op jit(solution)/shard_map/ppermute | solution.py:223
  100.9 32.0 %collective-permute-start.1 = (bf16[2,320,512]{2,1,0:T(8,128)(2,1)}, bf16[2,320,512]{2,1,0:T(8,128)(2,1)}, u32[]{:S(2)}, u32[]{:S(2)}) collective-permute-start(bf16[2,320,512]{2,1,0:T(8,128)(2,1)} %get-tuple-element.23), channel_id=1, source_target_pairs={{0,32},{16,48},{32,64},{48,80},{64,96},{80,112},{96,0},{112,16},{1... | collective-permute-start | bytes 1966088 | tf_op jit(solution)/shard_map/ppermute | solution.py:223
  135.9 1.7 %copy-start = (bf16[16,192,512]{2,1,0:T(8,128)(2,1)}, bf16[16,192,512]{2,1,0:T(8,128)(2,1)S(1)}, u32[]{:S(2)}) copy-start(bf16[16,192,512]{2,1,0:T(8,128)(2,1)S(1)} %all-to-all-done.1.refs_4_) | copy-start | bytes 9437188
  141.4 5.2 %collective-permute-start.4 = (bf16[8,192,512]{2,1,0:T(8,128)(2,1)}, bf16[8,192,512]{2,1,0:T(8,128)(2,1)S(1)}, u32[]{:S(2)}, u32[]{:S(2)}) collective-permute-start(bf16[8,192,512]{2,1,0:T(8,128)(2,1)} %get-tuple-element.22), channel_id=1, source_target_pairs={{0,16},{16,0},{32,48},{48,32},{64,80},{80,64},{96,112},{112,96},{1... | collective-permute-start | bytes 4718600 | tf_op jit(solution)/shard_map/ppermute | solution.py:217
  148.4 21.5 %copy-start.2 = (bf16[2,320,512]{2,1,0:T(8,128)(2,1)S(1)}, bf16[2,320,512]{2,1,0:T(8,128)(2,1)}, u32[]{:S(2)}) copy-start(bf16[2,320,512]{2,1,0:T(8,128)(2,1)} %select_convert_fusion) | copy-start | bytes 1966084
  148.5 10.4 %collective-permute-start.7 = (bf16[2,192,512]{2,1,0:T(8,128)(2,1)S(1)}, bf16[2,192,512]{2,1,0:T(8,128)(2,1)S(1)}, u32[]{:S(2)}, u32[]{:S(2)}) collective-permute-start(bf16[2,192,512]{2,1,0:T(8,128)(2,1)S(1)} %get-tuple-element.27), channel_id=1, source_target_pairs={{0,96},{16,112},{32,0},{48,16},{64,32},{80,48},{96,64},{112,80},{1... | collective-permute-start | bytes 1179656 | tf_op jit(solution)/shard_map/ppermute | solution.py:223
  148.6 12.0 %collective-permute-start.6 = (bf16[2,192,512]{2,1,0:T(8,128)(2,1)S(1)}, bf16[2,192,512]{2,1,0:T(8,128)(2,1)S(1)}, u32[]{:S(2)}, u32[]{:S(2)}) collective-permute-start(bf16[2,192,512]{2,1,0:T(8,128)(2,1)S(1)} %get-tuple-element.28), channel_id=1, source_target_pairs={{0,64},{16,80},{32,96},{48,112},{64,0},{80,16},{96,32},{112,48},{1... | collective-permute-start | bytes 1179656 | tf_op jit(solution)/shard_map/ppermute | solution.py:223
  149.6 20.0 %collective-permute-start.5 = (bf16[2,192,512]{2,1,0:T(8,128)(2,1)S(1)}, bf16[2,192,512]{2,1,0:T(8,128)(2,1)S(1)}, u32[]{:S(2)}, u32[]{:S(2)}) collective-permute-start(bf16[2,192,512]{2,1,0:T(8,128)(2,1)S(1)} %get-tuple-element.26), channel_id=1, source_target_pairs={{0,32},{16,48},{32,64},{48,80},{64,96},{80,112},{96,0},{112,16},{1... | collective-permute-start | bytes 1179656 | tf_op jit(solution)/shard_map/ppermute | solution.py:223

commit v3 on v2

--- a/solution.py
+++ b/solution.py
@@ -7,10 +7,11 @@
 from jax.experimental.pallas import tpu as pltpu
 from jax.sharding import PartitionSpec as P
 
-CHUNKS = (320, 192)
+CHUNKS = (400, 112)
 F32 = jnp.float32
 BF16 = jnp.bfloat16
 MIB = 1024 * 1024
+AHEAD = 4
 HBM = pl.BlockSpec(memory_space=pl.ANY)
 
 
@@ -42,20 +43,25 @@
 
     for_even, for_odd = lax.fori_loop(0, sectors, scan, (jnp.int32(0), jnp.int32(0)))
 
-    def fetch(i, count):
-        source = ls[i]
+    def pick(i, count):
         wanted = jnp.where((lp[i] & 1) == 1, for_odd, for_even)
-        need = (wanted == 1) & ((lp[source] & 1) != col_parity)
+        need = (wanted == 1) & ((lp[ls[i]] & 1) != col_parity)
 
         @pl.when(need)
         def _():
             items[count] = i
-            pltpu.make_async_copy(psi.at[source], pbuf.at[count], psem.at[count]).start()
-            pltpu.make_async_copy(left.at[i], lbuf.at[count], lsem.at[count]).start()
 
         return count + need.astype(jnp.int32)
 
-    count = lax.fori_loop(0, sectors, fetch, jnp.int32(0))
+    count = lax.fori_loop(0, sectors, pick, jnp.int32(0))
+
+    def fetch(j, carry=0):
+        i = items[j]
+        pltpu.make_async_copy(psi.at[ls[i]], pbuf.at[j], psem.at[j]).start()
+        pltpu.make_async_copy(left.at[i], lbuf.at[j], lsem.at[j]).start()
+        return carry
+
+    lax.fori_loop(0, jnp.minimum(count, AHEAD), fetch, 0)
 
     def stores(j):
         at = 0
@@ -66,6 +72,10 @@
             at += rows
 
     def work(j, carry):
+        @pl.when(j + AHEAD < count)
+        def _():
+            fetch(j + AHEAD)
+
         pltpu.make_async_copy(psi.at[0], pbuf.at[j], psem.at[j]).wait()
         pltpu.make_async_copy(left.at[0], lbuf.at[j], lsem.at[j]).wait()
         obuf[j] = jnp.dot(lbuf[j], pbuf[j], preferred_element_type=F32).astype(BF16)
@@ -107,13 +117,10 @@
     )(*lists, psi, left)
 
 
-def right_kernel(first, *refs):
-    lists, (block, right, keep, give), refs = refs[:4], refs[4:8], refs[8:]
-    if first:
-        turned, refs = refs[0], refs[1:]
-    held, (list_sem, items, zbuf, sbuf, rbuf, obuf, ssem, rsem, osem), refs = refs[:4], refs[4:13], refs[13:]
-    if first:
-        tbuf, tsem = refs
+def right_kernel(whole, *refs):
+    n = 7 if whole else 8
+    lists, (block, right), outs, refs = refs[:4], refs[4:6], refs[6:n], refs[n:]
+    held, (list_sem, items, zbuf, sbuf, rbuf, obuf, ssem, rsem, osem) = refs[:4], refs[4:]
     read_lists(lists, held, list_sem)
     ls, rs, lp, rp = held
     sectors = right.shape[0]
@@ -123,6 +130,10 @@
     zbuf[...] = jnp.zeros_like(zbuf)
 
     def place(buf, k):
+        if whole:
+            pltpu.make_async_copy(buf, outs[0].at[k], osem.at[k]).start()
+            return
+        keep, give = outs
         slot = (k // 4) * 2 + k % 2
         mine = (k // 2) % 2 == core
 
@@ -134,16 +145,13 @@
         def _():
             pltpu.make_async_copy(buf, give.at[slot], osem.at[k]).start()
 
-    def fetch(k, count):
+    def pick(k, count):
         live = (rp[k] & 1) != row_parity
-        source = rs[k]
-        need = live & ((rp[source] & 1) != source_parity)
+        need = live & ((rp[rs[k]] & 1) != source_parity)
 
         @pl.when(need)
         def _():
             items[count] = k
-            pltpu.make_async_copy(block.at[source], sbuf.at[count], ssem.at[count]).start()
-            pltpu.make_async_copy(right.at[k], rbuf.at[count], rsem.at[count]).start()
 
         @pl.when(live & jnp.logical_not(need))
         def _():
@@ -151,16 +159,26 @@
 
         return count + need.astype(jnp.int32)
 
-    count = lax.fori_loop(0, sectors, fetch, jnp.int32(0))
+    count = lax.fori_loop(0, sectors, pick, jnp.int32(0))
+
+    def fetch(j, carry=0):
+        k = items[j]
+        pltpu.make_async_copy(right.at[k], rbuf.at[j], rsem.at[j]).start()
+        pltpu.make_async_copy(block.at[rs[k]], sbuf.at[j], ssem.at[j]).start()
+        return carry
+
+    lax.fori_loop(0, jnp.minimum(count, AHEAD), fetch, 0)
 
     def work(j, carry):
+        @pl.when(j + AHEAD < count)
+        def _():
+            fetch(j + AHEAD)
+
         pltpu.make_async_copy(right.at[0], rbuf.at[j], rsem.at[j]).wait()
-        if first:
-            tbuf[j] = rbuf[j].T
-            pltpu.make_async_copy(tbuf.at[j], turned.at[items[j]], tsem.at[j]).start()
         pltpu.make_async_copy(block.at[0], sbuf.at[j], ssem.at[j]).wait()
-        factor = tbuf[j] if first else rbuf[j]
-        obuf[j] = jnp.dot(sbuf[j], factor, preferred_element_type=F32).astype(BF16)
+        obuf[j] = lax.dot_general(
+            sbuf[j], rbuf[j], (((1,), (1,)), ((), ())), preferred_element_type=F32
+        ).astype(BF16)
         place(obuf.at[j], items[j])
         return carry
 
@@ -169,28 +187,20 @@
     def finish(k, carry):
         @pl.when((rp[k] & 1) != row_parity)
         def _():
-            pltpu.make_async_copy(zbuf, keep.at[0], osem.at[k]).wait()
+            pltpu.make_async_copy(zbuf, outs[0].at[0], osem.at[k]).wait()
 
         return carry
 
     lax.fori_loop(0, sectors, finish, 0)
-    if first:
-        def turn(j, carry):
-            pltpu.make_async_copy(tbuf.at[j], turned.at[0], tsem.at[j]).wait()
-            return carry
-
-        lax.fori_loop(0, count, turn, 0)
-
-
-def right_products(lists, block, right, first):
+
+
+def right_products(lists, block, right, whole):
     k, rows, m = block.shape
     out = [jax.ShapeDtypeStruct((k // 2, rows, m), BF16)] * 2
-    extra = []
-    if first:
-        out = out + [jax.ShapeDtypeStruct((k, m, m), BF16)]
-        extra = [pltpu.VMEM((k, m, m), BF16), pltpu.SemaphoreType.DMA((k,))]
+    if whole:
+        out = [jax.ShapeDtypeStruct((k, rows, m), BF16)]
     return pl.pallas_call(
-        functools.partial(right_kernel, first),
+        functools.partial(right_kernel, whole),
         out_shape=out,
         in_specs=[HBM] * 6,
         out_specs=[HBM] * len(out),
@@ -203,8 +213,8 @@
             pltpu.SemaphoreType.DMA((k,)),
             pltpu.SemaphoreType.DMA((k,)),
             pltpu.SemaphoreType.DMA((k,)),
-        ] + extra,
-        compiler_params=pltpu.CompilerParams(vmem_limit_bytes=56 * MIB),
+        ],
+        compiler_params=pltpu.CompilerParams(vmem_limit_bytes=61 * MIB),
         cost_estimate=pl.CostEstimate(
             flops=16 * rows * m * m, bytes_accessed=8 * m * m * 2 + 16 * rows * m * 2, transcendentals=0
         ),
@@ -218,7 +228,7 @@
     pair = (keep.astype(F32) + got.astype(F32)).astype(BF16)
     chip = lax.axis_index("ops") // 2
     total = lax.dynamic_slice_in_dim(pair, chip * 2, 2).astype(F32)
-    for hop in (1, 2, 3):
+    for hop in (2, 1, 3):
         part = lax.dynamic_slice_in_dim(pair, (chip + hop) % 4 * 2, 2)
         part = lax.ppermute(part, "ops", [(o, (o + 2 * hop) % n) for o in range(n)])
         total = total + part.astype(F32)
@@ -233,12 +243,12 @@
     live = ((out_parity + row_parity) % 2 == 1)[:, None, None]
     sends = left_products(lists, psi[:, 0], left_ops[0])
     blocks = [lax.all_to_all(send, "sec", 0, 0, tiled=True) for send in sends]
-    keep, give, turned = right_products(lists, blocks[0], right_ops[0], True)
-    early = jnp.where(live, summed_over_ops(keep, give), 0.0).astype(BF16)
-    early, last = lax.optimization_barrier((early, blocks[1]))
-    keep, give = right_products(lists, last, turned, False)
-    late = jnp.where(live, summed_over_ops(keep, give), 0.0).astype(BF16)
-    return jnp.concatenate([early, late], axis=1)[None]
+    (partial,) = right_products(lists, blocks[0], right_ops[0], True)
+    early = lax.psum_scatter(partial, "ops", scatter_dimension=0, tiled=True)
+    keep, give = right_products(lists, blocks[1], right_ops[0], False)
+    late = summed_over_ops(keep, give).astype(BF16)
+    result = jnp.concatenate([early, late], axis=1)
+    return jnp.where(live, result, jnp.zeros_like(result))[None]
 
 
 def solution(mesh):

time: 174 us -> 168 us (0.966); the launches traced: 171 us -> 168 us
  blocking collectives: 68.6 us -> 119 us
  waiting for transfers between devices: 52.7 us -> 11.3 us
  between operations: 0.19 us -> 13.5 us
  starting transfers between devices: 19 us -> 7.67 us
  Pallas kernels: 15.2 us -> 9.82 us
  other arithmetic: 9.97 us -> 4.78 us
  local copies, waits for them, and re-layouts: 5.26 us -> 2.13 us
    all_to_all x1 -> x2, blocking collectives: 68.6 us -> 119 us  [local(): blocks = [lax.all_to_all(send, 'sec', 0, 0, tiled=True) for send in sends]]
    ppermute x6 -> x3, waiting for transfers between devices: 49.5 us -> 8.89 us  [summed_over_ops(): part = lax.ppermute(part, 'ops', [(o, (o + 2 * hop) % n) for o in range(n)])]
    all_to_all x1 -> x0, starting transfers between devices: 10.1 us -> none  [local(): blocks = [lax.all_to_all(send, 'sec', 0, 0, tiled=True) for send in sends]]
    pallas_call x1, Pallas kernels: 7.04 us -> 1.69 us  [left_products(): pl.pallas_call(left_kernel, out_shape=[jax.ShapeDtypeStruct((k, rows, m),...]
    convert_element_type x2 -> x1, other arithmetic: 5.17 us -> 1.45 us  [summed_over_ops(): pair = (keep.astype(F32) + got.astype(F32)).astype(BF16)]
    ppermute x2 -> x1, starting transfers between devices: 5.88 us -> 2.47 us  [summed_over_ops(): got = lax.ppermute(give, 'ops', [(o, o ^ 1) for o in range(n)])]
    convert_element_type x2 -> x0, other arithmetic: 3.13 us -> none  [the longest x1 2.9 us: local(): early = jnp.where(live, summed_over_ops(keep, give), 0.0).astype(BF16)]
    select_n x0 -> x1, other arithmetic: none -> 2.47 us  [local(): return jnp.where(live, result, jnp.zeros_like(result))[None]]
  transfers between devices with their start and end apart: 9 -> 5, of which waited for: 7 -> 4; matrix products, arithmetic and copies ran while one was open for 5% -> 2% of each run, Pallas kernels for 0% -> 2%
where the time goes in v3:
time: 168 us
  blocking collectives  119 us (71%)
  between operations  13.5 us (8%)
  waiting for transfers between devices  11.3 us (7%)
  Pallas kernels  9.82 us (6%)
  starting transfers between devices  7.67 us (5%)
  other arithmetic  4.78 us (3%)
  local copies, waits for them, and re-layouts  2.13 us (1%)
    all_to_all x2, blocking collectives, local(): blocks = [lax.all_to_all(send, 'sec', 0, 0, tiled=True) for send in sends]  119 us
    ppermute x3, waiting for transfers between devices, summed_over_ops(): part = lax.ppermute(part, 'ops', [(o, (o + 2 * hop) % n) for o in range(n)])  8.89 us
    pallas_call x2, Pallas kernels, right_products(): pl.pallas_call(functools.partial(right_kernel, whole), out_shape=out, in_...  8.12 us
    ppermute x3, starting transfers between devices, summed_over_ops(): part = lax.ppermute(part, 'ops', [(o, (o + 2 * hop) % n) for o in range(n)])  5.2 us
  transfers between devices with their start and end apart: 5, of which 4 were waited for; matrix products, arithmetic and copies ran while one was open for 2% of the time, Pallas kernels for 2%

profile of v3, /device:TPU:1, one launch (start us, length us, event | category | flops | bytes accessed | tf_op | source)
XLA Modules:
  0.0 167.6 jit_solution(8223018452772313813)
XLA Ops:
  6.5 0.0 reduce-scatter.2.cloned.1.call-start
  6.5 1.7 %left_products.1 = (bf16[16,400,512]{2,1,0:T(8,128)(2,1)}, bf16[16,112,512]{2,1,0:T(8,128)(2,1)}) custom-call(s32[16]{0:T(128)} %bitcast.14, s32[16]{0:T(128)} %bitcast.17, s32[16]{0:T(128)} %refs_2_.5, s32[16]{0:T(128)} %refs_3_.5, bf16[16,512,512]{2,1,0:T(8,128)(2,1)} %bitcast.11, bf16[16,512,512]{2,1,0:T(8,128)(2,1)} %bitcast.12), custom_call_target="tpu_custom_call" | custom-call | flops 1073741824 | bytes 6291456 | tf_op jit(solution)/shard_map/left_products/pallas_call | solution.py:98
  8.2 88.8 %all_to_all.10.refs_4_ = bf16[16,400,512]{2,1,0:T(8,128)(2,1)} all-to-all(bf16[16,400,512]{2,1,0:T(8,128)(2,1)} %get-tuple-element.9), channel_id=1, replica_groups=mesh['ops'=8,'sec'=16] {'sec'}, dimensions={0} | all-to-all | bytes 13107200 | tf_op jit(solution)/shard_map/all_to_all | solution.py:245
  97.1 4.5 %right_products.2 = bf16[16,400,512]{2,1,0:T(8,128)(2,1)} custom-call(s32[16]{0:T(128)} %bitcast.15, s32[16]{0:T(128)} %bitcast.18, s32[16]{0:T(128)} %refs_2_.5, s32[16]{0:T(128)} %refs_3_.5, bf16[16,400,512]{2,1,0:T(8,128)(2,1)} %all_to_all.10.refs_4_, bf16[16,512,512]{2,1,0:T(8,128)(2,1)} %bitcast.9), custom_call_target="tpu_custom_call" | custom-call | flops 1677721600 | bytes 10747904 | tf_op jit(solution)/shard_map/right_products/pallas_call | solution.py:202
  101.6 0.0 copy-start
  101.6 0.0 reduce-scatter.2.cloned.1.call-update
  101.6 1.5 copy-done
  103.1 29.7 %all_to_all.11.refs_4_ = bf16[16,112,512]{2,1,0:T(8,128)(2,1)} all-to-all(bf16[16,112,512]{2,1,0:T(8,128)(2,1)S(1)} %copy-done), channel_id=1, replica_groups=mesh['ops'=8,'sec'=16] {'sec'}, dimensions={0} | all-to-all | bytes 3670016 | tf_op jit(solution)/shard_map/all_to_all | solution.py:245
  132.7 3.6 %right_products.3 = (bf16[8,112,512]{2,1,0:T(8,128)(2,1)}, bf16[8,112,512]{2,1,0:T(8,128)(2,1)}) custom-call(s32[16]{0:T(128)} %bitcast.16, s32[16]{0:T(128)} %bitcast.19, s32[16]{0:T(128)} %refs_2_.5, s32[16]{0:T(128)} %refs_3_.5, bf16[16,112,512]{2,1,0:T(8,128)(2,1)} %all_to_all.11.refs_4_, bf16[16,512,512]{2,1,0:T(8,128)(2,1)} %bitcast.10), custom_call_target="tpu_custom_call" | custom-call | flops 469762048 | bytes 6029312 | tf_op jit(solution)/shard_map/right_products/pallas_call | solution.py:202
  136.4 2.5 %collective-permute-start = (bf16[8,112,512]{2,1,0:T(8,128)(2,1)}, bf16[8,112,512]{2,1,0:T(8,128)(2,1)S(1)}, u32[]{:S(2)}, u32[]{:S(2)}) collective-permute-start(bf16[8,112,512]{2,1,0:T(8,128)(2,1)} %get-tuple-element.12), channel_id=1, source_target_pairs={{0,16},{16,0},{32,48},{48,32},{64,80},{80,64},{96,112},{112,96},{1... | collective-permute-start | bytes 2752520 | tf_op jit(solution)/shard_map/ppermute | solution.py:227
  138.9 0.0 copy-start.2
  138.9 0.0 copy-start.1
  138.9 2.3 %collective-permute-done = bf16[8,112,512]{2,1,0:T(8,128)(2,1)S(1)} collective-permute-done((bf16[8,112,512]{2,1,0:T(8,128)(2,1)}, bf16[8,112,512]{2,1,0:T(8,128)(2,1)S(1)}, u32[]{:S(2)}, u32[]{:S(2)}) %collective-permute-start) | collective-permute-done | bytes 917536 | tf_op jit(solution)/shard_map/ppermute | solution.py:227
  141.2 1.4 add_convert_fusion
  142.7 0.1 constant_dynamic-slice_fusion.2
  142.7 2.5 %collective-permute-start.1 = (bf16[2,112,512]{2,1,0:T(8,128)(2,1)S(1)}, bf16[2,112,512]{2,1,0:T(8,128)(2,1)S(1)}, u32[]{:S(2)}, u32[]{:S(2)}) collective-permute-start(bf16[2,112,512]{2,1,0:T(8,128)(2,1)S(1)} %get-tuple-element.13), channel_id=1, source_target_pairs={{0,64},{16,80},{32,96},{48,112},{64,0},{80,16},{96,32},{112,48},{1... | collective-permute-start | bytes 688136 | tf_op jit(solution)/shard_map/ppermute | solution.py:233
  145.3 2.6 %collective-permute-start.2 = (bf16[2,112,512]{2,1,0:T(8,128)(2,1)S(1)}, bf16[2,112,512]{2,1,0:T(8,128)(2,1)S(1)}, u32[]{:S(2)}, u32[]{:S(2)}) collective-permute-start(bf16[2,112,512]{2,1,0:T(8,128)(2,1)S(1)} %get-tuple-element.15), channel_id=1, source_target_pairs={{0,32},{16,48},{32,64},{48,80},{64,96},{80,112},{96,0},{112,16},{1... | collective-permute-start | bytes 688136 | tf_op jit(solution)/shard_map/ppermute | solution.py:233
  147.8 0.1 collective-permute-start.3
  147.9 0.0 copy-done.2
  147.9 0.6 dynamic_slice.19
  148.5 0.0 copy-done.1
  148.5 0.7 fusion.1
  149.3 2.2 %collective-permute-done.1 = bf16[2,112,512]{2,1,0:T(8,128)(2,1)S(1)} collective-permute-done((bf16[2,112,512]{2,1,0:T(8,128)(2,1)S(1)}, bf16[2,112,512]{2,1,0:T(8,128)(2,1)S(1)}, u32[]{:S(2)}, u32[]{:S(2)}) %collective-permute-start.1) | collective-permute-done | bytes 229408 | tf_op jit(solution)/shard_map/ppermute | solution.py:233
  151.4 5.4 %collective-permute-done.2 = bf16[2,112,512]{2,1,0:T(8,128)(2,1)S(1)} collective-permute-done((bf16[2,112,512]{2,1,0:T(8,128)(2,1)S(1)}, bf16[2,112,512]{2,1,0:T(8,128)(2,1)S(1)}, u32[]{:S(2)}, u32[]{:S(2)}) %collective-permute-start.2) | collective-permute-done | bytes 229408 | tf_op jit(solution)/shard_map/ppermute | solution.py:233
  156.9 1.3 collective-permute-done.3
  158.1 0.1 fusion
  158.3 0.0 reduce-scatter.2.cloned.1.call-done
  158.3 2.5 %maximum_select_fusion = bf16[1,2,512,512]{3,2,1,0:T(8,128)(2,1)} fusion(bf16[1,2,112,512]{3,2,1,0:T(8,128)(2,1)S(1)} %fusion, bf16[1,2,400,512]{3,2,1,0:T(8,128)(2,1)} %bitcast.13, pred[2]{0:T(512)(128)(4,1)S(1)} %fusion.1), kind=kLoop, calls=%fused_computation.1 | loop fusion | flops 2621440 | bytes 2097154 | tf_op jit(solution)/shard_map/jit(_where)/select_n | solution.py:251
Async XLA Ops:
  6.5 151.8 %reduce-scatter.2.cloned.1.call-start = ((), (), s32[]{:S(2)}) async-start(), calls=%async_computation.3 | async-start | bytes 7372800 | tf_op jit(solution)/shard_map/reduce_scatter | solution.py:247
  101.6 1.5 copy-start
  136.4 4.8 %collective-permute-start = (bf16[8,112,512]{2,1,0:T(8,128)(2,1)}, bf16[8,112,512]{2,1,0:T(8,128)(2,1)S(1)}, u32[]{:S(2)}, u32[]{:S(2)}) collective-permute-start(bf16[8,112,512]{2,1,0:T(8,128)(2,1)} %get-tuple-element.12), channel_id=1, source_target_pairs={{0,16},{16,0},{32,48},{48,32},{64,80},{80,64},{96,112},{112,96},{1... | collective-permute-start | bytes 2752520 | tf_op jit(solution)/shard_map/ppermute | solution.py:227
  138.9 9.1 %copy-start.2 = (s32[16]{0:T(128)S(1)}, s32[16]{0:T(128)}, u32[]{:S(2)}) copy-start(s32[16]{0:T(128)} %refs_2_.5) | copy-start | bytes 196
  138.9 9.7 %copy-start.1 = (s32[16]{0:T(128)S(1)}, s32[16]{0:T(128)}, u32[]{:S(2)}) copy-start(s32[16]{0:T(128)} %refs_3_.5) | copy-start | bytes 196
  142.7 8.7 %collective-permute-start.1 = (bf16[2,112,512]{2,1,0:T(8,128)(2,1)S(1)}, bf16[2,112,512]{2,1,0:T(8,128)(2,1)S(1)}, u32[]{:S(2)}, u32[]{:S(2)}) collective-permute-start(bf16[2,112,512]{2,1,0:T(8,128)(2,1)S(1)} %get-tuple-element.13), channel_id=1, source_target_pairs={{0,64},{16,80},{32,96},{48,112},{64,0},{80,16},{96,32},{112,48},{1... | collective-permute-start | bytes 688136 | tf_op jit(solution)/shard_map/ppermute | solution.py:233
  145.3 11.6 %collective-permute-start.2 = (bf16[2,112,512]{2,1,0:T(8,128)(2,1)S(1)}, bf16[2,112,512]{2,1,0:T(8,128)(2,1)S(1)}, u32[]{:S(2)}, u32[]{:S(2)}) collective-permute-start(bf16[2,112,512]{2,1,0:T(8,128)(2,1)S(1)} %get-tuple-element.15), channel_id=1, source_target_pairs={{0,32},{16,48},{32,64},{48,80},{64,96},{80,112},{96,0},{112,16},{1... | collective-permute-start | bytes 688136 | tf_op jit(solution)/shard_map/ppermute | solution.py:233
  147.8 10.3 %collective-permute-start.3 = (bf16[2,112,512]{2,1,0:T(8,128)(2,1)S(1)}, bf16[2,112,512]{2,1,0:T(8,128)(2,1)S(1)}, u32[]{:S(2)}, u32[]{:S(2)}) collective-permute-start(bf16[2,112,512]{2,1,0:T(8,128)(2,1)S(1)} %get-tuple-element.14), channel_id=1, source_target_pairs={{0,96},{16,112},{32,0},{48,16},{64,32},{80,48},{96,64},{112,80},{1... | collective-permute-start | bytes 688136 | tf_op jit(solution)/shard_map/ppermute | solution.py:233
Sparse Core Ops, SparseCore 0:
  101.7 45.5 reduce-scatter.1

commit v4 on v3

--- a/solution.py
+++ b/solution.py
@@ -27,9 +27,33 @@
     return [pltpu.SMEM((k,), jnp.int32)] * 4 + [pltpu.SemaphoreType.DMA((4,))]
 
 
+def note(need, item, source, carry, items, slots, fresh, seen):
+    count, used = carry
+    known = seen[source]
+    new = (need & (known == 0)).astype(jnp.int32)
+
+    @pl.when(need)
+    def _():
+        slot = jnp.where(known == 0, used, known - 1)
+        items[count] = item
+        slots[count] = slot
+        fresh[count] = new
+        seen[source] = slot + 1
+
+    return count + need.astype(jnp.int32), used + new
+
+
+def forget(seen, sectors):
+    def clear(r, carry):
+        seen[r] = 0
+        return carry
+
+    lax.fori_loop(0, sectors, clear, 0)
+
+
 def left_kernel(*refs):
     lists, (psi, left), outs = refs[:4], refs[4:6], refs[6 : 6 + len(CHUNKS)]
-    held, list_sem, items, pbuf, lbuf, obuf, psem, lsem, osem = refs[6 + len(CHUNKS):][:4], *refs[10 + len(CHUNKS):]
+    held, list_sem, items, slots, fresh, seen, pbuf, lbuf, obuf, psem, lsem, osem = refs[6 + len(CHUNKS):][:4], *refs[10 + len(CHUNKS):]
     read_lists(lists, held, list_sem)
     ls, rs, lp, rp = held
     sectors = psi.shape[0]
@@ -43,21 +67,22 @@
 
     for_even, for_odd = lax.fori_loop(0, sectors, scan, (jnp.int32(0), jnp.int32(0)))
 
-    def pick(i, count):
+    forget(seen, sectors)
+
+    def pick(i, carry):
         wanted = jnp.where((lp[i] & 1) == 1, for_odd, for_even)
         need = (wanted == 1) & ((lp[ls[i]] & 1) != col_parity)
-
-        @pl.when(need)
-        def _():
-            items[count] = i
-
-        return count + need.astype(jnp.int32)
-
-    count = lax.fori_loop(0, sectors, pick, jnp.int32(0))
+        return note(need, i, ls[i], carry, items, slots, fresh, seen)
+
+    count, _ = lax.fori_loop(0, sectors, pick, (jnp.int32(0), jnp.int32(0)))
 
     def fetch(j, carry=0):
         i = items[j]
-        pltpu.make_async_copy(psi.at[ls[i]], pbuf.at[j], psem.at[j]).start()
+
+        @pl.when(fresh[j] == 1)
+        def _():
+            pltpu.make_async_copy(psi.at[ls[i]], pbuf.at[slots[j]], psem.at[slots[j]]).start()
+
         pltpu.make_async_copy(left.at[i], lbuf.at[j], lsem.at[j]).start()
         return carry
 
@@ -76,9 +101,12 @@
         def _():
             fetch(j + AHEAD)
 
-        pltpu.make_async_copy(psi.at[0], pbuf.at[j], psem.at[j]).wait()
+        @pl.when(fresh[j] == 1)
+        def _():
+            pltpu.make_async_copy(psi.at[0], pbuf.at[slots[j]], psem.at[slots[j]]).wait()
+
         pltpu.make_async_copy(left.at[0], lbuf.at[j], lsem.at[j]).wait()
-        obuf[j] = jnp.dot(lbuf[j], pbuf[j], preferred_element_type=F32).astype(BF16)
+        obuf[j] = jnp.dot(lbuf[j], pbuf[slots[j]], preferred_element_type=F32).astype(BF16)
         for copy in stores(j):
             copy.start()
         return carry
@@ -102,6 +130,9 @@
         out_specs=[HBM] * len(CHUNKS),
         scratch_shapes=list_scratch(k) + [
             pltpu.SMEM((k,), jnp.int32),
+            pltpu.SMEM((k,), jnp.int32),
+            pltpu.SMEM((k,), jnp.int32),
+            pltpu.SMEM((k,), jnp.int32),
             pltpu.VMEM((k, m, m), BF16),
             pltpu.VMEM((k, m, m), BF16),
             pltpu.VMEM((k, m, m), BF16),
@@ -120,7 +151,7 @@
 def right_kernel(whole, *refs):
     n = 7 if whole else 8
     lists, (block, right), outs, refs = refs[:4], refs[4:6], refs[6:n], refs[n:]
-    held, (list_sem, items, zbuf, sbuf, rbuf, obuf, ssem, rsem, osem) = refs[:4], refs[4:]
+    held, (list_sem, items, slots, fresh, seen, zbuf, sbuf, rbuf, obuf, ssem, rsem, osem) = refs[:4], refs[4:]
     read_lists(lists, held, list_sem)
     ls, rs, lp, rp = held
     sectors = right.shape[0]
@@ -145,26 +176,28 @@
         def _():
             pltpu.make_async_copy(buf, give.at[slot], osem.at[k]).start()
 
-    def pick(k, count):
+    forget(seen, sectors)
+
+    def pick(k, carry):
         live = (rp[k] & 1) != row_parity
         need = live & ((rp[rs[k]] & 1) != source_parity)
 
-        @pl.when(need)
-        def _():
-            items[count] = k
-
         @pl.when(live & jnp.logical_not(need))
         def _():
             place(zbuf, k)
 
-        return count + need.astype(jnp.int32)
-
-    count = lax.fori_loop(0, sectors, pick, jnp.int32(0))
+        return note(need, k, rs[k], carry, items, slots, fresh, seen)
+
+    count, _ = lax.fori_loop(0, sectors, pick, (jnp.int32(0), jnp.int32(0)))
 
     def fetch(j, carry=0):
         k = items[j]
         pltpu.make_async_copy(right.at[k], rbuf.at[j], rsem.at[j]).start()
-        pltpu.make_async_copy(block.at[rs[k]], sbuf.at[j], ssem.at[j]).start()
+
+        @pl.when(fresh[j] == 1)
+        def _():
+            pltpu.make_async_copy(block.at[rs[k]], sbuf.at[slots[j]], ssem.at[slots[j]]).start()
+
         return carry
 
     lax.fori_loop(0, jnp.minimum(count, AHEAD), fetch, 0)
@@ -175,9 +208,13 @@
             fetch(j + AHEAD)
 
         pltpu.make_async_copy(right.at[0], rbuf.at[j], rsem.at[j]).wait()
-        pltpu.make_async_copy(block.at[0], sbuf.at[j], ssem.at[j]).wait()
+
+        @pl.when(fresh[j] == 1)
+        def _():
+            pltpu.make_async_copy(block.at[0], sbuf.at[slots[j]], ssem.at[slots[j]]).wait()
+
         obuf[j] = lax.dot_general(
-            sbuf[j], rbuf[j], (((1,), (1,)), ((), ())), preferred_element_type=F32
+            sbuf[slots[j]], rbuf[j], (((1,), (1,)), ((), ())), preferred_element_type=F32
         ).astype(BF16)
         place(obuf.at[j], items[j])
         return carry
@@ -206,6 +243,9 @@
         out_specs=[HBM] * len(out),
         scratch_shapes=list_scratch(k) + [
             pltpu.SMEM((k,), jnp.int32),
+            pltpu.SMEM((k,), jnp.int32),
+            pltpu.SMEM((k,), jnp.int32),
+            pltpu.SMEM((k,), jnp.int32),
             pltpu.VMEM((rows, m), BF16),
             pltpu.VMEM((k, rows, m), BF16),
             pltpu.VMEM((k, m, m), BF16),
@@ -246,9 +286,10 @@
     (partial,) = right_products(lists, blocks[0], right_ops[0], True)
     early = lax.psum_scatter(partial, "ops", scatter_dimension=0, tiled=True)
     keep, give = right_products(lists, blocks[1], right_ops[0], False)
-    late = summed_over_ops(keep, give).astype(BF16)
-    result = jnp.concatenate([early, late], axis=1)
-    return jnp.where(live, result, jnp.zeros_like(result))[None]
+    late = jnp.where(live, summed_over_ops(keep, give), 0.0).astype(BF16)
+    early = jnp.where(live, early, jnp.zeros_like(early))
+    early = lax.optimization_barrier(jnp.pad(early, ((0, 0), (0, CHUNKS[1]), (0, 0))))
+    return lax.dynamic_update_slice(early, late, (0, CHUNKS[0], 0))[None]
 
 
 def solution(mesh):

time: 168 us -> 168 us (level); the launches traced: 168 us -> 166 us
  Pallas kernels: 9.82 us -> 19.7 us
  blocking collectives: 119 us -> 112 us
  waiting for transfers between devices: 11.3 us -> 8.02 us
  starting transfers between devices: 7.67 us -> 5.17 us
    pallas_call x1, Pallas kernels: 1.69 us -> 9.3 us  [left_products(): pl.pallas_call(left_kernel, out_shape=[jax.ShapeDtypeStruct((k, rows, m),...]
    all_to_all x2, blocking collectives: 119 us -> 112 us  [local(): blocks = [lax.all_to_all(send, 'sec', 0, 0, tiled=True) for send in sends]]
    pallas_call x2, Pallas kernels: 8.12 us -> 10.4 us  [right_products(): pl.pallas_call(functools.partial(right_kernel, whole), out_shape=out, in_...]
    ppermute x1, starting transfers between devices: 2.47 us -> 0.58 us  [summed_over_ops(): got = lax.ppermute(give, 'ops', [(o, o ^ 1) for o in range(n)])]
    ppermute x3, waiting for transfers between devices: 8.89 us -> 7.13 us  [summed_over_ops(): part = lax.ppermute(part, 'ops', [(o, (o + 2 * hop) % n) for o in range(n)])]
  transfers between devices with their start and end apart: 5 -> 5, of which waited for: 4 -> 3; matrix products, arithmetic and copies ran while one was open for 2% -> 3% of each run, Pallas kernels for 2% -> 3%
where the time goes in v4:
time: 168 us; the launch traced here: 166 us
  blocking collectives  112 us (67%)
  Pallas kernels  19.7 us (12%)
  between operations  13.4 us (8%)
  waiting for transfers between devices  8.02 us (5%)
  starting transfers between devices  5.17 us (3%)
  other arithmetic  4.32 us (3%)
  local copies, waits for them, and re-layouts  3.24 us (2%)
    all_to_all x2, blocking collectives, local(): blocks = [lax.all_to_all(send, 'sec', 0, 0, tiled=True) for send in sends]  112 us
    pallas_call x2, Pallas kernels, right_products(): pl.pallas_call(functools.partial(right_kernel, whole), out_shape=out, in_...  10.4 us
    pallas_call x1, Pallas kernels, left_products(): pl.pallas_call(left_kernel, out_shape=[jax.ShapeDtypeStruct((k, rows, m),...  9.3 us
    ppermute x3, waiting for transfers between devices, summed_over_ops(): part = lax.ppermute(part, 'ops', [(o, (o + 2 * hop) % n) for o in range(n)])  7.13 us
    ppermute x3, starting transfers between devices, summed_over_ops(): part = lax.ppermute(part, 'ops', [(o, (o + 2 * hop) % n) for o in range(n)])  4.59 us
  transfers between devices with their start and end apart: 5, of which 3 were waited for; matrix products, arithmetic and copies ran while one was open for 3% of the time, Pallas kernels for 3%

profile of v4, /device:TPU:1, one launch (start us, length us, event | category | flops | bytes accessed | tf_op | source)
XLA Modules:
  0.0 165.7 jit_solution(6643546153365100068)
XLA Ops:
  6.5 0.0 reduce-scatter.2.cloned.1.call-start
  6.5 9.3 %left_products.1 = (bf16[16,400,512]{2,1,0:T(8,128)(2,1)}, bf16[16,112,512]{2,1,0:T(8,128)(2,1)}) custom-call(s32[16]{0:T(128)} %bitcast.16, s32[16]{0:T(128)} %bitcast.19, s32[16]{0:T(128)} %refs_2_.5, s32[16]{0:T(128)} %refs_3_.5, bf16[16,512,512]{2,1,0:T(8,128)(2,1)} %bitcast.13, bf16[16,512,512]{2,1,0:T(8,128)(2,1)} %bitcast.14), custom_call_target="tpu_custom_call" | custom-call | flops 1073741824 | bytes 6291456 | tf_op jit(solution)/shard_map/left_products/pallas_call | solution.py:126
  15.8 83.1 %all_to_all.10.refs_4_ = bf16[16,400,512]{2,1,0:T(8,128)(2,1)} all-to-all(bf16[16,400,512]{2,1,0:T(8,128)(2,1)} %get-tuple-element.9), channel_id=1, replica_groups=mesh['ops'=8,'sec'=16] {'sec'}, dimensions={0} | all-to-all | bytes 13107200 | tf_op jit(solution)/shard_map/all_to_all | solution.py:285
  98.9 5.6 %right_products.2 = bf16[16,400,512]{2,1,0:T(8,128)(2,1)} custom-call(s32[16]{0:T(128)} %bitcast.17, s32[16]{0:T(128)} %bitcast.20, s32[16]{0:T(128)} %refs_2_.5, s32[16]{0:T(128)} %refs_3_.5, bf16[16,400,512]{2,1,0:T(8,128)(2,1)} %all_to_all.10.refs_4_, bf16[16,512,512]{2,1,0:T(8,128)(2,1)} %bitcast.11), custom_call_target="tpu_custom_call" | custom-call | flops 1677721600 | bytes 10747904 | tf_op jit(solution)/shard_map/right_products/pallas_call | solution.py:239
  104.6 0.0 copy-start
  104.6 0.0 reduce-scatter.2.cloned.1.call-update
  104.6 1.5 copy-done
  106.1 0.0 copy-start.2
  106.1 0.0 copy-start.1
  106.1 28.8 %all_to_all.11.refs_4_ = bf16[16,112,512]{2,1,0:T(8,128)(2,1)} all-to-all(bf16[16,112,512]{2,1,0:T(8,128)(2,1)S(1)} %copy-done), channel_id=1, replica_groups=mesh['ops'=8,'sec'=16] {'sec'}, dimensions={0} | all-to-all | bytes 3670016 | tf_op jit(solution)/shard_map/all_to_all | solution.py:285
  134.9 4.7 %right_products.3 = (bf16[8,112,512]{2,1,0:T(8,128)(2,1)}, bf16[8,112,512]{2,1,0:T(8,128)(2,1)}) custom-call(s32[16]{0:T(128)} %bitcast.18, s32[16]{0:T(128)} %bitcast.21, s32[16]{0:T(128)} %refs_2_.5, s32[16]{0:T(128)} %refs_3_.5, bf16[16,112,512]{2,1,0:T(8,128)(2,1)} %all_to_all.11.refs_4_, bf16[16,512,512]{2,1,0:T(8,128)(2,1)} %bitcast.12), custom_call_target="tpu_custom_call" | custom-call | flops 469762048 | bytes 6029312 | tf_op jit(solution)/shard_map/right_products/pallas_call | solution.py:239
  139.6 0.6 collective-permute-start
  140.2 0.0 copy-done.2
  140.2 0.7 dynamic_slice.19
  140.8 0.0 copy-done.1
  140.8 0.8 fusion.2
  141.6 0.9 collective-permute-done
  142.5 1.5 add_convert_fusion
  143.9 0.1 constant_dynamic-slice_fusion.2
  144.0 1.9 %collective-permute-start.1 = (bf16[2,112,512]{2,1,0:T(8,128)(2,1)S(1)}, bf16[2,112,512]{2,1,0:T(8,128)(2,1)S(1)}, u32[]{:S(2)}, u32[]{:S(2)}) collective-permute-start(bf16[2,112,512]{2,1,0:T(8,128)(2,1)S(1)} %get-tuple-element.13), channel_id=1, source_target_pairs={{0,64},{16,80},{32,96},{48,112},{64,0},{80,16},{96,32},{112,48},{1... | collective-permute-start | bytes 688136 | tf_op jit(solution)/shard_map/ppermute | solution.py:273
  145.9 0.0 collective-permute-start.2
  145.9 2.7 %collective-permute-start.3 = (bf16[2,112,512]{2,1,0:T(8,128)(2,1)S(1)}, bf16[2,112,512]{2,1,0:T(8,128)(2,1)S(1)}, u32[]{:S(2)}, u32[]{:S(2)}) collective-permute-start(bf16[2,112,512]{2,1,0:T(8,128)(2,1)S(1)} %get-tuple-element.14), channel_id=1, source_target_pairs={{0,96},{16,112},{32,0},{48,16},{64,32},{80,48},{96,64},{112,80},{1... | collective-permute-start | bytes 688136 | tf_op jit(solution)/shard_map/ppermute | solution.py:273
  148.6 0.0 reduce-scatter.2.cloned.1.call-done
  148.6 1.3 broadcast_select_fusion
  149.9 1.0 pad.4
  150.9 1.6 collective-permute-done.1
  152.5 5.6 %collective-permute-done.2 = bf16[2,112,512]{2,1,0:T(8,128)(2,1)S(1)} collective-permute-done((bf16[2,112,512]{2,1,0:T(8,128)(2,1)S(1)}, bf16[2,112,512]{2,1,0:T(8,128)(2,1)S(1)}, u32[]{:S(2)}, u32[]{:S(2)}) %collective-permute-start.2) | collective-permute-done | bytes 229408 | tf_op jit(solution)/shard_map/ppermute | solution.py:273
  158.1 0.0 collective-permute-done.3
  158.1 0.8 fusion.1
Async XLA Ops:
  6.5 142.1 %reduce-scatter.2.cloned.1.call-start = ((), (), s32[]{:S(2)}) async-start(), calls=%async_computation.3 | async-start | bytes 7372800 | tf_op jit(solution)/shard_map/reduce_scatter | solution.py:287
  104.6 1.5 copy-start
  106.1 34.1 %copy-start.2 = (s32[16]{0:T(128)S(1)}, s32[16]{0:T(128)}, u32[]{:S(2)}) copy-start(s32[16]{0:T(128)} %refs_2_.5) | copy-start | bytes 196
  106.1 34.8 %copy-start.1 = (s32[16]{0:T(128)S(1)}, s32[16]{0:T(128)}, u32[]{:S(2)}) copy-start(s32[16]{0:T(128)} %refs_3_.5) | copy-start | bytes 196
  139.6 2.9 %collective-permute-start = (bf16[8,112,512]{2,1,0:T(8,128)(2,1)}, bf16[8,112,512]{2,1,0:T(8,128)(2,1)S(1)}, u32[]{:S(2)}, u32[]{:S(2)}) collective-permute-start(bf16[8,112,512]{2,1,0:T(8,128)(2,1)} %get-tuple-element.12), channel_id=1, source_target_pairs={{0,16},{16,0},{32,48},{48,32},{64,80},{80,64},{96,112},{112,96},{1... | collective-permute-start | bytes 2752520 | tf_op jit(solution)/shard_map/ppermute | solution.py:267
  144.0 8.5 %collective-permute-start.1 = (bf16[2,112,512]{2,1,0:T(8,128)(2,1)S(1)}, bf16[2,112,512]{2,1,0:T(8,128)(2,1)S(1)}, u32[]{:S(2)}, u32[]{:S(2)}) collective-permute-start(bf16[2,112,512]{2,1,0:T(8,128)(2,1)S(1)} %get-tuple-element.13), channel_id=1, source_target_pairs={{0,64},{16,80},{32,96},{48,112},{64,0},{80,16},{96,32},{112,48},{1... | collective-permute-start | bytes 688136 | tf_op jit(solution)/shard_map/ppermute | solution.py:273
  145.9 12.1 %collective-permute-start.2 = (bf16[2,112,512]{2,1,0:T(8,128)(2,1)S(1)}, bf16[2,112,512]{2,1,0:T(8,128)(2,1)S(1)}, u32[]{:S(2)}, u32[]{:S(2)}) collective-permute-start(bf16[2,112,512]{2,1,0:T(8,128)(2,1)S(1)} %get-tuple-element.15), channel_id=1, source_target_pairs={{0,32},{16,48},{32,64},{48,80},{64,96},{80,112},{96,0},{112,16},{1... | collective-permute-start | bytes 688136 | tf_op jit(solution)/shard_map/ppermute | solution.py:273
  145.9 12.1 %collective-permute-start.3 = (bf16[2,112,512]{2,1,0:T(8,128)(2,1)S(1)}, bf16[2,112,512]{2,1,0:T(8,128)(2,1)S(1)}, u32[]{:S(2)}, u32[]{:S(2)}) collective-permute-start(bf16[2,112,512]{2,1,0:T(8,128)(2,1)S(1)} %get-tuple-element.14), channel_id=1, source_target_pairs={{0,96},{16,112},{32,0},{48,16},{64,32},{80,48},{96,64},{112,80},{1... | collective-permute-start | bytes 688136 | tf_op jit(solution)/shard_map/ppermute | solution.py:273
Sparse Core Ops, SparseCore 0:
  104.7 40.4 reduce-scatter.1

commit v5 on v4

--- a/solution.py
+++ b/solution.py
@@ -48,7 +48,7 @@
         seen[r] = 0
         return carry
 
-    lax.fori_loop(0, sectors, clear, 0)
+    lax.fori_loop(0, sectors, clear, 0, unroll=True)
 
 
 def left_kernel(*refs):
@@ -65,7 +65,7 @@
         odd = rp[k] & 1
         return flags[0] | (hit * odd), flags[1] | (hit * (1 - odd))
 
-    for_even, for_odd = lax.fori_loop(0, sectors, scan, (jnp.int32(0), jnp.int32(0)))
+    for_even, for_odd = lax.fori_loop(0, sectors, scan, (jnp.int32(0), jnp.int32(0)), unroll=True)
 
     forget(seen, sectors)
 
@@ -74,7 +74,7 @@
         need = (wanted == 1) & ((lp[ls[i]] & 1) != col_parity)
         return note(need, i, ls[i], carry, items, slots, fresh, seen)
 
-    count, _ = lax.fori_loop(0, sectors, pick, (jnp.int32(0), jnp.int32(0)))
+    count, _ = lax.fori_loop(0, sectors, pick, (jnp.int32(0), jnp.int32(0)), unroll=True)
 
     def fetch(j, carry=0):
         i = items[j]
@@ -188,7 +188,7 @@
 
         return note(need, k, rs[k], carry, items, slots, fresh, seen)
 
-    count, _ = lax.fori_loop(0, sectors, pick, (jnp.int32(0), jnp.int32(0)))
+    count, _ = lax.fori_loop(0, sectors, pick, (jnp.int32(0), jnp.int32(0)), unroll=True)
 
     def fetch(j, carry=0):
         k = items[j]
@@ -228,7 +228,7 @@
 
         return carry
 
-    lax.fori_loop(0, sectors, finish, 0)
+    lax.fori_loop(0, sectors, finish, 0, unroll=True)
 
 
 def right_products(lists, block, right, whole):

time: 168 us -> 166 us (0.988); the launches traced: 166 us -> 166 us
  starting transfers between devices: 5.17 us -> 10.6 us
  Pallas kernels: 19.7 us -> 15.4 us
    pallas_call x1, Pallas kernels: 9.3 us -> 5.29 us  [left_products(): pl.pallas_call(left_kernel, out_shape=[jax.ShapeDtypeStruct((k, rows, m),...]
    ppermute x3, starting transfers between devices: 4.59 us -> 7.9 us  [summed_over_ops(): part = lax.ppermute(part, 'ops', [(o, (o + 2 * hop) % n) for o in range(n)])]
    ppermute x1, starting transfers between devices: 0.58 us -> 2.71 us  [summed_over_ops(): got = lax.ppermute(give, 'ops', [(o, o ^ 1) for o in range(n)])]
where the time goes in v5:
time: 166 us
  blocking collectives  112 us (67%)
  Pallas kernels  15.4 us (9%)
  between operations  13.4 us (8%)
  starting transfers between devices  10.6 us (6%)
  waiting for transfers between devices  6.88 us (4%)
  other arithmetic  4.3 us (3%)
  local copies, waits for them, and re-layouts  3.24 us (2%)
    all_to_all x2, blocking collectives, local(): blocks = [lax.all_to_all(send, 'sec', 0, 0, tiled=True) for send in sends]  112 us
    pallas_call x2, Pallas kernels, right_products(): pl.pallas_call(functools.partial(right_kernel, whole), out_shape=out, in_...  10.1 us
    ppermute x3, starting transfers between devices, summed_over_ops(): part = lax.ppermute(part, 'ops', [(o, (o + 2 * hop) % n) for o in range(n)])  7.9 us
    ppermute x3, waiting for transfers between devices, summed_over_ops(): part = lax.ppermute(part, 'ops', [(o, (o + 2 * hop) % n) for o in range(n)])  5.99 us
    pallas_call x1, Pallas kernels, left_products(): pl.pallas_call(left_kernel, out_shape=[jax.ShapeDtypeStruct((k, rows, m),...  5.29 us
  transfers between devices with their start and end apart: 5, of which 3 were waited for; matrix products, arithmetic and copies ran while one was open for 3% of the time, Pallas kernels for 3%

profile of v5, /device:TPU:1, one launch (start us, length us, event | category | flops | bytes accessed | tf_op | source)
XLA Modules:
  0.0 165.9 jit_solution(16338508859394791425)
XLA Ops:
  6.5 0.0 reduce-scatter.2.cloned.1.call-start
  6.5 5.3 %left_products.1 = (bf16[16,400,512]{2,1,0:T(8,128)(2,1)}, bf16[16,112,512]{2,1,0:T(8,128)(2,1)}) custom-call(s32[16]{0:T(128)} %bitcast.16, s32[16]{0:T(128)} %bitcast.19, s32[16]{0:T(128)} %refs_2_.5, s32[16]{0:T(128)} %refs_3_.5, bf16[16,512,512]{2,1,0:T(8,128)(2,1)} %bitcast.13, bf16[16,512,512]{2,1,0:T(8,128)(2,1)} %bitcast.14), custom_call_target="tpu_custom_call" | custom-call | flops 1073741824 | bytes 6291456 | tf_op jit(solution)/shard_map/left_products/pallas_call | solution.py:126
  11.8 85.7 %all_to_all.10.refs_4_ = bf16[16,400,512]{2,1,0:T(8,128)(2,1)} all-to-all(bf16[16,400,512]{2,1,0:T(8,128)(2,1)} %get-tuple-element.9), channel_id=1, replica_groups=mesh['ops'=8,'sec'=16] {'sec'}, dimensions={0} | all-to-all | bytes 13107200 | tf_op jit(solution)/shard_map/all_to_all | solution.py:285
  97.5 5.6 %right_products.2 = bf16[16,400,512]{2,1,0:T(8,128)(2,1)} custom-call(s32[16]{0:T(128)} %bitcast.17, s32[16]{0:T(128)} %bitcast.20, s32[16]{0:T(128)} %refs_2_.5, s32[16]{0:T(128)} %refs_3_.5, bf16[16,400,512]{2,1,0:T(8,128)(2,1)} %all_to_all.10.refs_4_, bf16[16,512,512]{2,1,0:T(8,128)(2,1)} %bitcast.11), custom_call_target="tpu_custom_call" | custom-call | flops 1677721600 | bytes 10747904 | tf_op jit(solution)/shard_map/right_products/pallas_call | solution.py:239
  103.1 0.0 copy-start
  103.2 0.0 reduce-scatter.2.cloned.1.call-update
  103.2 1.5 copy-done
  104.7 0.0 copy-start.2
  104.7 0.0 copy-start.1
  104.7 26.3 %all_to_all.11.refs_4_ = bf16[16,112,512]{2,1,0:T(8,128)(2,1)} all-to-all(bf16[16,112,512]{2,1,0:T(8,128)(2,1)S(1)} %copy-done), channel_id=1, replica_groups=mesh['ops'=8,'sec'=16] {'sec'}, dimensions={0} | all-to-all | bytes 3670016 | tf_op jit(solution)/shard_map/all_to_all | solution.py:285
  130.9 4.5 %right_products.3 = (bf16[8,112,512]{2,1,0:T(8,128)(2,1)}, bf16[8,112,512]{2,1,0:T(8,128)(2,1)}) custom-call(s32[16]{0:T(128)} %bitcast.18, s32[16]{0:T(128)} %bitcast.21, s32[16]{0:T(128)} %refs_2_.5, s32[16]{0:T(128)} %refs_3_.5, bf16[16,112,512]{2,1,0:T(8,128)(2,1)} %all_to_all.11.refs_4_, bf16[16,512,512]{2,1,0:T(8,128)(2,1)} %bitcast.12), custom_call_target="tpu_custom_call" | custom-call | flops 469762048 | bytes 6029312 | tf_op jit(solution)/shard_map/right_products/pallas_call | solution.py:239
  135.5 2.7 %collective-permute-start = (bf16[8,112,512]{2,1,0:T(8,128)(2,1)}, bf16[8,112,512]{2,1,0:T(8,128)(2,1)S(1)}, u32[]{:S(2)}, u32[]{:S(2)}) collective-permute-start(bf16[8,112,512]{2,1,0:T(8,128)(2,1)} %get-tuple-element.12), channel_id=1, source_target_pairs={{0,16},{16,0},{32,48},{48,32},{64,80},{80,64},{96,112},{112,96},{1... | collective-permute-start | bytes 2752520 | tf_op jit(solution)/shard_map/ppermute | solution.py:267
  138.2 0.0 copy-done.2
  138.2 0.7 dynamic_slice.19
  138.8 0.0 copy-done.1
  138.9 0.8 fusion.2
  139.6 0.9 collective-permute-done
  140.5 1.4 add_convert_fusion
  141.9 0.1 constant_dynamic-slice_fusion.2
  142.0 5.2 %collective-permute-start.1 = (bf16[2,112,512]{2,1,0:T(8,128)(2,1)S(1)}, bf16[2,112,512]{2,1,0:T(8,128)(2,1)S(1)}, u32[]{:S(2)}, u32[]{:S(2)}) collective-permute-start(bf16[2,112,512]{2,1,0:T(8,128)(2,1)S(1)} %get-tuple-element.13), channel_id=1, source_target_pairs={{0,64},{16,80},{32,96},{48,112},{64,0},{80,16},{96,32},{112,48},{1... | collective-permute-start | bytes 688136 | tf_op jit(solution)/shard_map/ppermute | solution.py:273
  147.2 0.2 collective-permute-start.2
  147.5 2.4 %collective-permute-start.3 = (bf16[2,112,512]{2,1,0:T(8,128)(2,1)S(1)}, bf16[2,112,512]{2,1,0:T(8,128)(2,1)S(1)}, u32[]{:S(2)}, u32[]{:S(2)}) collective-permute-start(bf16[2,112,512]{2,1,0:T(8,128)(2,1)S(1)} %get-tuple-element.14), channel_id=1, source_target_pairs={{0,96},{16,112},{32,0},{48,16},{64,32},{80,48},{96,64},{112,80},{1... | collective-permute-start | bytes 688136 | tf_op jit(solution)/shard_map/ppermute | solution.py:273
  149.9 0.0 reduce-scatter.2.cloned.1.call-done
  149.9 1.3 broadcast_select_fusion
  151.2 1.0 pad.4
  152.2 0.7 collective-permute-done.1
  152.9 5.3 %collective-permute-done.2 = bf16[2,112,512]{2,1,0:T(8,128)(2,1)S(1)} collective-permute-done((bf16[2,112,512]{2,1,0:T(8,128)(2,1)S(1)}, bf16[2,112,512]{2,1,0:T(8,128)(2,1)S(1)}, u32[]{:S(2)}, u32[]{:S(2)}) %collective-permute-start.2) | collective-permute-done | bytes 229408 | tf_op jit(solution)/shard_map/ppermute | solution.py:273
  158.2 0.0 collective-permute-done.3
  158.2 0.8 fusion.1
Async XLA Ops:
  6.5 143.4 %reduce-scatter.2.cloned.1.call-start = ((), (), s32[]{:S(2)}) async-start(), calls=%async_computation.3 | async-start | bytes 7372800 | tf_op jit(solution)/shard_map/reduce_scatter | solution.py:287
  103.1 1.5 copy-start
  104.7 33.5 %copy-start.2 = (s32[16]{0:T(128)S(1)}, s32[16]{0:T(128)}, u32[]{:S(2)}) copy-start(s32[16]{0:T(128)} %refs_2_.5) | copy-start | bytes 196
  104.7 34.2 %copy-start.1 = (s32[16]{0:T(128)S(1)}, s32[16]{0:T(128)}, u32[]{:S(2)}) copy-start(s32[16]{0:T(128)} %refs_3_.5) | copy-start | bytes 196
  135.5 5.0 %collective-permute-start = (bf16[8,112,512]{2,1,0:T(8,128)(2,1)}, bf16[8,112,512]{2,1,0:T(8,128)(2,1)S(1)}, u32[]{:S(2)}, u32[]{:S(2)}) collective-permute-start(bf16[8,112,512]{2,1,0:T(8,128)(2,1)} %get-tuple-element.12), channel_id=1, source_target_pairs={{0,16},{16,0},{32,48},{48,32},{64,80},{80,64},{96,112},{112,96},{1... | collective-permute-start | bytes 2752520 | tf_op jit(solution)/shard_map/ppermute | solution.py:267
  142.0 10.9 %collective-permute-start.1 = (bf16[2,112,512]{2,1,0:T(8,128)(2,1)S(1)}, bf16[2,112,512]{2,1,0:T(8,128)(2,1)S(1)}, u32[]{:S(2)}, u32[]{:S(2)}) collective-permute-start(bf16[2,112,512]{2,1,0:T(8,128)(2,1)S(1)} %get-tuple-element.13), channel_id=1, source_target_pairs={{0,64},{16,80},{32,96},{48,112},{64,0},{80,16},{96,32},{112,48},{1... | collective-permute-start | bytes 688136 | tf_op jit(solution)/shard_map/ppermute | solution.py:273
  147.2 11.0 %collective-permute-start.2 = (bf16[2,112,512]{2,1,0:T(8,128)(2,1)S(1)}, bf16[2,112,512]{2,1,0:T(8,128)(2,1)S(1)}, u32[]{:S(2)}, u32[]{:S(2)}) collective-permute-start(bf16[2,112,512]{2,1,0:T(8,128)(2,1)S(1)} %get-tuple-element.15), channel_id=1, source_target_pairs={{0,32},{16,48},{32,64},{48,80},{64,96},{80,112},{96,0},{112,16},{1... | collective-permute-start | bytes 688136 | tf_op jit(solution)/shard_map/ppermute | solution.py:273
  147.5 10.7 %collective-permute-start.3 = (bf16[2,112,512]{2,1,0:T(8,128)(2,1)S(1)}, bf16[2,112,512]{2,1,0:T(8,128)(2,1)S(1)}, u32[]{:S(2)}, u32[]{:S(2)}) collective-permute-start(bf16[2,112,512]{2,1,0:T(8,128)(2,1)S(1)} %get-tuple-element.14), channel_id=1, source_target_pairs={{0,96},{16,112},{32,0},{48,16},{64,32},{80,48},{96,64},{112,80},{1... | collective-permute-start | bytes 688136 | tf_op jit(solution)/shard_map/ppermute | solution.py:273
Sparse Core Ops, SparseCore 0:
  103.3 42.0 reduce-scatter.1
